TPU v7x, 256 devices: a whole 4x4x8 slice. The times are simulated.
256 devices in a mesh: seq: 64 (over z, x, y_lo), chan: 4 (over y_hi, core).
Axes of the slice: x: 4, y: 4 (y_hi: 2, y_lo: 2; y = y_hi * 2 + y_lo), z: 8, core: 2. Of those that a mesh axis runs over, the one named last changes fastest.
Arguments:
- query_input: bfloat16 [256, 32768], P('chan', 'seq'), may hold values from -6 to 6
- key_input: bfloat16 [256, 32768], P('chan', 'seq'), may hold values from -6 to 6
- value_input: bfloat16 [256, 32768], P('chan', 'seq'), may hold values from -6 to 6
- long_filter: float32 [64, 32768], P('chan', 'seq'), may hold values from -3 to 3
- query_taps: float32 [3, 256], P(None, 'chan'), may hold values from -3 to 3
- key_taps: float32 [3, 256], P(None, 'chan'), may hold values from -3 to 3
- value_taps: float32 [3, 256], P(None, 'chan'), may hold values from -3 to 3
- skip_gain: float32 [256], P('chan'), may hold values from -3 to 3
- out_cotangent: bfloat16 [256, 32768], P('chan', 'seq'), may hold values from -6 to 6
Outputs:
- gated_output: bfloat16 [256, 32768], P('chan', 'seq')
- query_gradient: bfloat16 [256, 32768], P('chan', 'seq')
- key_gradient: bfloat16 [256, 32768], P('chan', 'seq')
- value_gradient: bfloat16 [256, 32768], P('chan', 'seq')
All inputs are finite; a program needn't handle non-finite values.
Results may differ from a plain program's by a relative error of at most 0.00175.
Values may be sent and summed in bfloat16 or wider, within the bound.
A program may use at most 128 MiB of HBM per device.

v0:
```python
import math

import jax
import jax.numpy as jnp
from jax import lax
from jax.sharding import PartitionSpec as P


def shifted(value, axis, steps):
    count = lax.axis_size(axis)
    leading, last = (max(0, -steps), min(count, count - steps))
    return lax.ppermute(value, axis, [(source, source + steps) for source in range(leading, last)])


def angle_table(numer, modulus):
    angles = (numer % modulus).astype(jnp.float32) * (-2.0 * math.pi / modulus)
    return (jnp.cos(angles), jnp.sin(angles))


def matmul(left, right):
    return jnp.dot(left, right, precision=lax.Precision.HIGHEST)


def block_dft(real, imag, inverse):
    full_shape = real.shape
    last_width = full_shape[-1]
    row_count = full_shape[-2]
    group_size = 1
    while group_size * 2 * last_width <= 128 and row_count % (group_size * 2) == 0:
        group_size = group_size * 2
    offsets = jnp.arange(last_width, dtype=jnp.int32)
    cosine, sine = angle_table(offsets[:, None] * offsets[None, :], last_width)
    if inverse:
        sine = -sine
    identity = jnp.eye(group_size, dtype=jnp.float32)
    cos_block = jnp.kron(identity, cosine)
    sin_block = jnp.kron(identity, sine)
    flat_re = real.reshape(-1, group_size * last_width)
    flat_im = imag.reshape(-1, group_size * last_width)
    out_re = matmul(flat_re, cos_block) - matmul(flat_im, sin_block)
    out_im = matmul(flat_re, sin_block) + matmul(flat_im, cos_block)
    return (out_re.reshape(full_shape), out_im.reshape(full_shape))


def forward_spectra(signal):
    devices = lax.axis_size("seq")
    own_index = lax.axis_index("seq")
    row_count, block_len = signal.shape
    sub_width = block_len // devices
    full_len = 2 * devices * block_len
    send = (
        signal.reshape(row_count, devices, sub_width)
        .transpose(1, 0, 2)
        .reshape(devices, row_count * sub_width)
    )
    received = lax.all_to_all(send, "seq", split_axis=0, concat_axis=0, tiled=True)
    outer = jnp.arange(devices, dtype=jnp.int32)
    doubled = jnp.arange(2 * devices, dtype=jnp.int32)
    inner = jnp.arange(sub_width, dtype=jnp.int32)
    cos_first, sin_first = angle_table(doubled[:, None] * outer[None, :], 2 * devices)
    first_re = matmul(cos_first, received).reshape(2 * devices, row_count, sub_width)
    first_im = matmul(sin_first, received).reshape(2 * devices, row_count, sub_width)
    cos_twist, sin_twist = angle_table(
        doubled[:, None] * (own_index * sub_width + inner)[None, :], full_len
    )
    cos_twist = cos_twist[:, None, :]
    sin_twist = sin_twist[:, None, :]
    twist_re = first_re * cos_twist - first_im * sin_twist
    twist_im = first_re * sin_twist + first_im * cos_twist
    got_re, got_im = (
        lax.all_to_all(
            twist_re.reshape(devices, -1), "seq", split_axis=0, concat_axis=0, tiled=True
        ),
        lax.all_to_all(
            twist_im.reshape(devices, -1), "seq", split_axis=0, concat_axis=0, tiled=True
        ),
    )
    cos_mid, sin_mid = angle_table(outer[:, None] * outer[None, :], devices)
    mid_re = matmul(cos_mid, got_re) - matmul(sin_mid, got_im)
    mid_im = matmul(cos_mid, got_im) + matmul(sin_mid, got_re)
    four_dims = (devices, 2, row_count, sub_width)
    mid_re = mid_re.reshape(four_dims)
    mid_im = mid_im.reshape(four_dims)
    cos_fine, sin_fine = angle_table(outer[:, None] * inner[None, :], block_len)
    cos_fine = cos_fine[:, None, None, :]
    sin_fine = sin_fine[:, None, None, :]
    fine_re = mid_re * cos_fine - mid_im * sin_fine
    fine_im = mid_re * sin_fine + mid_im * cos_fine
    return block_dft(fine_re, fine_im, False)


def inverse_signal(real, imag):
    devices = lax.axis_size("seq")
    own_index = lax.axis_index("seq")
    row_count = real.shape[2]
    sub_width = real.shape[3]
    block_len = devices * sub_width
    full_len = 2 * devices * block_len
    outer = jnp.arange(devices, dtype=jnp.int32)
    doubled = jnp.arange(2 * devices, dtype=jnp.int32)
    inner = jnp.arange(sub_width, dtype=jnp.int32)
    back_re, back_im = block_dft(real, imag, True)
    cos_fine, sin_fine = angle_table(outer[:, None] * inner[None, :], block_len)
    cos_fine = cos_fine[:, None, None, :]
    sin_fine = sin_fine[:, None, None, :]
    fine_re = (back_re * cos_fine + back_im * sin_fine).reshape(devices, -1)
    fine_im = (back_im * cos_fine - back_re * sin_fine).reshape(devices, -1)
    cos_mid, sin_mid = angle_table(outer[:, None] * outer[None, :], devices)
    mid_re = matmul(cos_mid, fine_re) + matmul(sin_mid, fine_im)
    mid_im = matmul(cos_mid, fine_im) - matmul(sin_mid, fine_re)
    got_re, got_im = (
        lax.all_to_all(mid_re, "seq", split_axis=0, concat_axis=0, tiled=True),
        lax.all_to_all(mid_im, "seq", split_axis=0, concat_axis=0, tiled=True),
    )
    got_re = got_re.reshape(2 * devices, row_count, sub_width)
    got_im = got_im.reshape(2 * devices, row_count, sub_width)
    cos_twist, sin_twist = angle_table(
        doubled[:, None] * (own_index * sub_width + inner)[None, :], full_len
    )
    cos_twist = cos_twist[:, None, :]
    sin_twist = sin_twist[:, None, :]
    twist_re = (got_re * cos_twist + got_im * sin_twist).reshape(2 * devices, -1)
    twist_im = (got_im * cos_twist - got_re * sin_twist).reshape(2 * devices, -1)
    cos_last, sin_last = angle_table(outer[:, None] * doubled[None, :], 2 * devices)
    result_rows = (matmul(cos_last, twist_re) + matmul(sin_last, twist_im)) * (1.0 / full_len)
    arrived = lax.all_to_all(result_rows, "seq", split_axis=0, concat_axis=0, tiled=True)
    return (
        arrived.reshape(devices, row_count, sub_width)
        .transpose(1, 0, 2)
        .reshape(row_count, block_len)
    )


def causal_taps(signal, edge, taps):
    extended = jnp.concatenate([edge, signal], axis=1).astype(jnp.float32)
    length_dev = signal.shape[1]
    return (
        taps[0][:, None] * extended[:, 2:]
        + taps[1][:, None] * extended[:, 1 : length_dev + 1]
        + taps[2][:, None] * extended[:, :length_dev]
    )


def reverse_taps(signal, edge, taps):
    extended = jnp.concatenate([signal, edge], axis=1)
    length_dev = signal.shape[1]
    return (
        taps[0][:, None] * extended[:, :length_dev]
        + taps[1][:, None] * extended[:, 1 : length_dev + 1]
        + taps[2][:, None] * extended[:, 2:]
    )


def body(
    query_input,
    key_input,
    value_input,
    long_filter,
    query_taps,
    key_taps,
    value_taps,
    skip_gain,
    out_cotangent,
):
    edge_q, edge_k, edge_v = shifted(
        (query_input[:, -2:], key_input[:, -2:], value_input[:, -2:]), "seq", 1
    )
    short_q = causal_taps(query_input, edge_q, query_taps)
    short_k = causal_taps(key_input, edge_k, key_taps)
    short_v = causal_taps(value_input, edge_v, value_taps)
    product = short_k * short_v
    cotangent = out_cotangent.astype(jnp.float32)
    grad_mixed = cotangent * short_q
    filter_block = lax.all_gather(long_filter, "chan", axis=0, tiled=True)
    filter_count = filter_block.shape[0]
    channel_rows = product.shape[0]
    spec_re, spec_im = forward_spectra(jnp.concatenate([filter_block, product, grad_mixed], axis=0))
    grad_re = spec_re[:, :, filter_count + channel_rows :]
    grad_im = spec_im[:, :, filter_count + channel_rows :]
    prod_re = spec_re[:, :, filter_count : filter_count + channel_rows]
    prod_im = spec_im[:, :, filter_count : filter_count + channel_rows]
    filt_re = spec_re[:, :, :filter_count]
    filt_im = spec_im[:, :, :filter_count]
    fwd_re = filt_re * prod_re - filt_im * prod_im
    fwd_im = filt_re * prod_im + filt_im * prod_re
    bwd_re = filt_re * grad_re + filt_im * grad_im
    bwd_im = filt_re * grad_im - filt_im * grad_re
    both = inverse_signal(
        jnp.concatenate([fwd_re, bwd_re], axis=2), jnp.concatenate([fwd_im, bwd_im], axis=2)
    )
    causal = both[:channel_rows]
    backward = both[channel_rows:]
    skip_col = skip_gain[:, None]
    mixed = causal + skip_col * product
    gated_output = (short_q * mixed).astype(jnp.bfloat16)
    grad_short_q = cotangent * mixed
    grad_product = backward + skip_col * grad_mixed
    grad_short_k = grad_product * short_v
    grad_short_v = grad_product * short_k
    next_q, next_k, next_v = shifted(
        (grad_short_q[:, :2], grad_short_k[:, :2], grad_short_v[:, :2]), "seq", -1
    )
    query_gradient = reverse_taps(grad_short_q, next_q, query_taps).astype(jnp.bfloat16)
    key_gradient = reverse_taps(grad_short_k, next_k, key_taps).astype(jnp.bfloat16)
    value_gradient = reverse_taps(grad_short_v, next_v, value_taps).astype(jnp.bfloat16)
    return (gated_output, query_gradient, key_gradient, value_gradient)


def solution(mesh):
    in_specs = (
        P("chan", "seq"),
        P("chan", "seq"),
        P("chan", "seq"),
        P("chan", "seq"),
        P(None, "chan"),
        P(None, "chan"),
        P(None, "chan"),
        P("chan"),
        P("chan", "seq"),
    )
    out_specs = (P("chan", "seq"), P("chan", "seq"), P("chan", "seq"), P("chan", "seq"))
    return jax.shard_map(body, mesh=mesh, in_specs=in_specs, out_specs=out_specs, check_vma=False)
```

profile of v0, /device:TPU:30, one launch (start us, length us, event | category | flops | bytes accessed | tf_op | source)
XLA Modules:
  0.0 296.7 jit_solution(4712727234056669662)
XLA Ops:
  1.6 3.9 %collective-permute-start.1 = (bf16[64,2]{0,1:T(2,128)(2,1)S(1)}, bf16[64,2]{0,1:T(2,128)(2,1)S(1)}, u32[]{:S(2)}, u32[]{:S(2)}) collective-permute-start(bf16[64,2]{0,1:T(2,128)(2,1)S(1)} %slice.173), channel_id=1, source_target_pairs={{0,4},{4,8},{8,12},{12,16},{16,20},{20,24},{24,28},{28,32},{32,36}... | collective-permute-start | bytes 776 | tf_op jit(solution)/shard_map/ppermute | solution.py:12
  6.5 3.2 %collective-permute-start.2 = (bf16[64,2]{0,1:T(2,128)(2,1)S(1)}, bf16[64,2]{0,1:T(2,128)(2,1)S(1)}, u32[]{:S(2)}, u32[]{:S(2)}) collective-permute-start(bf16[64,2]{0,1:T(2,128)(2,1)S(1)} %slice.177), channel_id=1, source_target_pairs={{0,4},{4,8},{8,12},{12,16},{16,20},{20,24},{24,28},{28,32},{32,36}... | collective-permute-start | bytes 776 | tf_op jit(solution)/shard_map/ppermute | solution.py:12
  10.7 3.6 %collective-permute-start = (bf16[64,2]{0,1:T(2,128)(2,1)S(1)}, bf16[64,2]{0,1:T(2,128)(2,1)S(1)}, u32[]{:S(2)}, u32[]{:S(2)}) collective-permute-start(bf16[64,2]{0,1:T(2,128)(2,1)S(1)} %slice.169), channel_id=1, source_target_pairs={{0,4},{4,8},{8,12},{12,16},{16,20},{20,24},{24,28},{28,32},{32,36}... | collective-permute-start | bytes 776 | tf_op jit(solution)/shard_map/ppermute | solution.py:12
  15.9 7.1 %all_gather.3 = f32[64,512]{1,0:T(8,128)S(1)} all-gather(f32[16,512]{1,0:T(8,128)} %param.12), channel_id=1, replica_groups=mesh['seq'=64,'chan'=4] {'chan'}, dimensions={0}, use_global_device_ids=true | all-gather | bytes 163840 | tf_op jit(solution)/shard_map/all_gather | solution.py:174
  27.9 11.7 %all-to-all-start = ((f32[64,1,1536]{2,1,0:T(1,128)}), f32[64,1,1536]{2,1,0:T(1,128)S(1)}, u32[]{:S(2)}, u32[]{:S(2)}) async-start(f32[64,1,1536]{2,1,0:T(1,128)} %copy.144), calls=%async_computation | async-start | bytes 786432 | tf_op jit(solution)/shard_map/all_to_all | solution.py:56
  39.7 14.3 %all-to-all-done = f32[64,1,1536]{2,1,0:T(1,128)S(1)} async-done(((f32[64,1,1536]{2,1,0:T(1,128)}), f32[64,1,1536]{2,1,0:T(1,128)S(1)}, u32[]{:S(2)}, u32[]{:S(2)}) %all-to-all-start) | async-done | bytes 393248 | tf_op jit(solution)/shard_map/all_to_all | solution.py:56
  54.8 1.4 fusion.60
  56.2 1.5 multiply_subtract_fusion.3
  57.7 6.9 %copy.148 = f32[128,192,8]{2,1,0:T(8,128)} copy(f32[128,192,8]{0,1,2:T(8,128)S(1)} %get-tuple-element.33) | data formatting | bytes 1572864 | tf_op jit(solution)/shard_map/sub | solution.py:68
  64.6 10.4 %all_to_all.57 = f32[64,1,3072]{2,1,0:T(1,128)} reshape(f32[128,192,8]{2,1,0:T(8,128)} %copy.148) | data formatting | bytes 1572864 | tf_op jit(solution)/shard_map/all_to_all | solution.py:71
  75.0 6.8 %all-to-all-start.1 = ((f32[64,1,3072]{2,1,0:T(1,128)}), f32[64,1,3072]{2,1,0:T(1,128)S(1)}, u32[]{:S(2)}, u32[]{:S(2)}) async-start(f32[64,1,3072]{2,1,0:T(1,128)} %all_to_all.57), calls=%async_computation.1 | async-start | bytes 1572864 | tf_op jit(solution)/shard_map/all_to_all | solution.py:71
  81.8 6.9 %copy.150 = f32[128,192,8]{2,1,0:T(8,128)} copy(f32[128,192,8]{0,1,2:T(8,128)S(1)} %get-tuple-element.34) | data formatting | bytes 1572864 | tf_op jit(solution)/shard_map/add | solution.py:69
  88.7 10.3 %all_to_all.58 = f32[64,1,3072]{2,1,0:T(1,128)} reshape(f32[128,192,8]{2,1,0:T(8,128)} %copy.150) | data formatting | bytes 1572864 | tf_op jit(solution)/shard_map/all_to_all | solution.py:74
  99.0 4.6 %all-to-all-done.1 = f32[64,1,3072]{2,1,0:T(1,128)S(1)} async-done(((f32[64,1,3072]{2,1,0:T(1,128)}), f32[64,1,3072]{2,1,0:T(1,128)S(1)}, u32[]{:S(2)}, u32[]{:S(2)}) %all-to-all-start.1) | async-done | bytes 786464 | tf_op jit(solution)/shard_map/all_to_all | solution.py:71
  103.7 7.0 %all-to-all-start.2 = ((f32[64,1,3072]{2,1,0:T(1,128)}), f32[64,1,3072]{2,1,0:T(1,128)S(1)}, u32[]{:S(2)}, u32[]{:S(2)}) async-start(f32[64,1,3072]{2,1,0:T(1,128)} %all_to_all.58), calls=%async_computation.2 | async-start | bytes 1572864 | tf_op jit(solution)/shard_map/all_to_all | solution.py:74
  110.9 1.3 copy.152
  112.3 1.3 copy.153
  113.8 1.8 broadcast_multiply_fusion
  115.6 1.6 mul.950
  117.2 2.3 mul.955
  120.9 11.1 %all-to-all-done.2 = f32[64,1,3072]{2,1,0:T(1,128)S(1)} async-done(((f32[64,1,3072]{2,1,0:T(1,128)}), f32[64,1,3072]{2,1,0:T(1,128)S(1)}, u32[]{:S(2)}, u32[]{:S(2)}) %all-to-all-start.2) | async-done | bytes 786464 | tf_op jit(solution)/shard_map/all_to_all | solution.py:74
  133.9 2.5 multiply_add_fusion.2
  137.5 1.6 fusion.171
  139.1 1.6 convolution_subtract_fusion.1
  140.7 8.6 %reshape.323 = f32[64,2,192,8]{3,2,1,0:T(8,128)} reshape(f32[1536,128]{1,0:T(8,128)S(1)} %convolution_subtract_fusion.1) | data formatting | bytes 1572864 | tf_op jit(solution)/shard_map/reshape | solution.py:42
  150.1 8.7 %reshape.324 = f32[64,2,192,8]{3,2,1,0:T(8,128)} reshape(f32[1536,128]{1,0:T(8,128)S(1)} %convolution_add_fusion.1) | data formatting | bytes 1572864 | tf_op jit(solution)/shard_map/reshape | solution.py:42
  158.8 22.4 %multiply_add_fusion = (f32[64,2,64,8]{3,2,1,0:T(8,128)S(1)}, f32[64,2,64,8]{3,2,1,0:T(8,128)S(1)}, f32[64,2,64,8]{3,2,1,0:T(8,128)}, f32[64,2,64,8]{3,2,1,0:T(8,128)}) fusion(f32[64,2,192,8]{3,2,1,0:T(8,128)} %reshape.324, f32[64,2,192,8]{3,2,1,0:T(8,128)} %reshape.323), kind=kLoop, calls=%fused_computation.3 | loop fusion | flops 786432 | bytes 2621440 | tf_op jit(solution)/shard_map/add | solution.py:185
  181.3 4.1 %pad_maximum_fusion.1 = f32[64,2,128,8]{3,2,1,0:T(8,128)} fusion(f32[64,2,64,8]{3,2,1,0:T(8,128)S(1)} %get-tuple-element.26, f32[64,2,64,8]{3,2,1,0:T(8,128)S(1)} %get-tuple-element.25), kind=kLoop, calls=%fused_computation.1 | loop fusion | flops 131072 | bytes 1048576 | tf_op jit(solution)/shard_map/concatenate | solution.py:189
  185.4 6.4 %reshape.326 = f32[1024,128]{1,0:T(8,128)S(1)} reshape(f32[64,2,128,8]{3,2,1,0:T(8,128)} %pad_maximum_fusion.1) | data formatting | bytes 1048576 | tf_op jit(solution)/shard_map/reshape | solution.py:39
  191.8 8.4 %pad_maximum_fusion = f32[64,2,128,8]{3,2,1,0:T(8,128)} fusion(f32[64,2,64,8]{3,2,1,0:T(8,128)} %get-tuple-element.27, f32[64,2,64,8]{3,2,1,0:T(8,128)} %get-tuple-element.28), kind=kLoop, calls=%fused_computation | loop fusion | flops 131072 | bytes 1048576 | tf_op jit(solution)/shard_map/concatenate | solution.py:189
  200.2 6.4 %reshape.325 = f32[1024,128]{1,0:T(8,128)S(1)} reshape(f32[64,2,128,8]{3,2,1,0:T(8,128)} %pad_maximum_fusion) | data formatting | bytes 1048576 | tf_op jit(solution)/shard_map/reshape | solution.py:38
  209.4 1.3 copy.156
  210.7 1.4 fusion.4
  212.2 1.4 fusion.81
  213.6 1.4 fusion
  214.9 1.4 copy.160
  216.3 6.8 %all-to-all-start.3 = ((f32[64,1,2048]{2,1,0:T(1,128)}), f32[64,1,2048]{2,1,0:T(1,128)S(1)}, u32[]{:S(2)}, u32[]{:S(2)}) async-start(f32[64,1,2048]{2,1,0:T(1,128)} %copy.160), calls=%async_computation.3 | async-start | bytes 1048576 | tf_op jit(solution)/shard_map/all_to_all | solution.py:112
  223.1 1.4 fusion.79
  224.5 1.4 fusion.1
  225.9 1.3 copy.162
  227.2 11.1 %all-to-all-done.3 = f32[64,1,2048]{2,1,0:T(1,128)S(1)} async-done(((f32[64,1,2048]{2,1,0:T(1,128)}), f32[64,1,2048]{2,1,0:T(1,128)S(1)}, u32[]{:S(2)}, u32[]{:S(2)}) %all-to-all-start.3) | async-done | bytes 524320 | tf_op jit(solution)/shard_map/all_to_all | solution.py:112
  238.3 6.8 %all-to-all-start.4 = ((f32[64,1,2048]{2,1,0:T(1,128)}), f32[64,1,2048]{2,1,0:T(1,128)S(1)}, u32[]{:S(2)}, u32[]{:S(2)}) async-start(f32[64,1,2048]{2,1,0:T(1,128)} %copy.162), calls=%async_computation.4 | async-start | bytes 1048576 | tf_op jit(solution)/shard_map/all_to_all | solution.py:113
  246.9 12.9 %all-to-all-done.4 = f32[64,1,2048]{2,1,0:T(1,128)S(1)} async-done(((f32[64,1,2048]{2,1,0:T(1,128)}), f32[64,1,2048]{2,1,0:T(1,128)S(1)}, u32[]{:S(2)}, u32[]{:S(2)}) %all-to-all-start.4) | async-done | bytes 524320 | tf_op jit(solution)/shard_map/all_to_all | solution.py:113
  262.7 16.3 %all_to_all.65 = f32[64,1,1024]{2,1,0:T(1,128)S(1)} all-to-all(f32[64,1,1024]{2,1,0:T(1,128)S(1)} %copy.166), channel_id=1, replica_groups=mesh['seq'=64,'chan'=4] {'seq'}, dimensions={0} | all-to-all | bytes 524288 | tf_op jit(solution)/shard_map/all_to_all | solution.py:126
  280.9 2.9 collective-permute-start.5
  283.8 3.4 %collective-permute-start.4 = (f32[64,2]{0,1:T(2,128)S(1)}, f32[64,2]{0,1:T(2,128)S(1)}, u32[]{:S(2)}, u32[]{:S(2)}) collective-permute-start(f32[64,2]{0,1:T(2,128)S(1)} %slice.192), channel_id=1, source_target_pairs={{4,0},{8,4},{12,8},{16,12},{20,16},{24,20},{28,24},{32,28},{36,32}... | collective-permute-start | bytes 1544 | tf_op jit(solution)/shard_map/ppermute | solution.py:12
  287.2 2.9 collective-permute-start.3
  293.8 1.8 collective-permute-done.3
  (119 shorter events, 29.3 us)
Async XLA Ops:
  1.6 23.5 %collective-permute-start.1 = (bf16[64,2]{0,1:T(2,128)(2,1)S(1)}, bf16[64,2]{0,1:T(2,128)(2,1)S(1)}, u32[]{:S(2)}, u32[]{:S(2)}) collective-permute-start(bf16[64,2]{0,1:T(2,128)(2,1)S(1)} %slice.173), channel_id=1, source_target_pairs={{0,4},{4,8},{8,12},{12,16},{16,20},{20,24},{24,28},{28,32},{32,36}... | collective-permute-start | bytes 776 | tf_op jit(solution)/shard_map/ppermute | solution.py:12
  6.5 18.6 %collective-permute-start.2 = (bf16[64,2]{0,1:T(2,128)(2,1)S(1)}, bf16[64,2]{0,1:T(2,128)(2,1)S(1)}, u32[]{:S(2)}, u32[]{:S(2)}) collective-permute-start(bf16[64,2]{0,1:T(2,128)(2,1)S(1)} %slice.177), channel_id=1, source_target_pairs={{0,4},{4,8},{8,12},{12,16},{16,20},{20,24},{24,28},{28,32},{32,36}... | collective-permute-start | bytes 776 | tf_op jit(solution)/shard_map/ppermute | solution.py:12
  10.7 13.5 %collective-permute-start = (bf16[64,2]{0,1:T(2,128)(2,1)S(1)}, bf16[64,2]{0,1:T(2,128)(2,1)S(1)}, u32[]{:S(2)}, u32[]{:S(2)}) collective-permute-start(bf16[64,2]{0,1:T(2,128)(2,1)S(1)} %slice.169), channel_id=1, source_target_pairs={{0,4},{4,8},{8,12},{12,16},{16,20},{20,24},{24,28},{28,32},{32,36}... | collective-permute-start | bytes 776 | tf_op jit(solution)/shard_map/ppermute | solution.py:12
  15.1 11.1 %copy-start.16 = (f32[64]{0:T(128)}, f32[64]{0:T(128)S(1)}, u32[]{:S(2)}) copy-start(f32[64]{0:T(128)S(1)} %get-tuple-element.50) | copy-start | bytes 772
  15.1 11.1 %copy-start.18 = (f32[64]{0:T(128)}, f32[64]{0:T(128)S(1)}, u32[]{:S(2)}) copy-start(f32[64]{0:T(128)S(1)} %get-tuple-element.51) | copy-start | bytes 772
  15.1 11.1 %copy-start.20 = (f32[64]{0:T(128)}, f32[64]{0:T(128)S(1)}, u32[]{:S(2)}) copy-start(f32[64]{0:T(128)S(1)} %get-tuple-element.52) | copy-start | bytes 772
  15.9 10.3 %copy-start.4 = (f32[64]{0:T(128)}, f32[64]{0:T(128)S(1)}, u32[]{:S(2)}) copy-start(f32[64]{0:T(128)S(1)} %get-tuple-element.57) | copy-start | bytes 772
  15.9 10.3 %copy-start.6 = (f32[64]{0:T(128)}, f32[64]{0:T(128)S(1)}, u32[]{:S(2)}) copy-start(f32[64]{0:T(128)S(1)} %get-tuple-element.58) | copy-start | bytes 772
  15.9 10.3 %copy-start.8 = (f32[64]{0:T(128)}, f32[64]{0:T(128)S(1)}, u32[]{:S(2)}) copy-start(f32[64]{0:T(128)S(1)} %get-tuple-element.59) | copy-start | bytes 772
  15.9 10.3 %copy-start.10 = (f32[64]{0:T(128)}, f32[64]{0:T(128)S(1)}, u32[]{:S(2)}) copy-start(f32[64]{0:T(128)S(1)} %get-tuple-element.47) | copy-start | bytes 772
  15.9 10.3 %copy-start.12 = (f32[64]{0:T(128)}, f32[64]{0:T(128)S(1)}, u32[]{:S(2)}) copy-start(f32[64]{0:T(128)S(1)} %get-tuple-element.48) | copy-start | bytes 772
  15.9 10.3 %copy-start.14 = (f32[64]{0:T(128)}, f32[64]{0:T(128)S(1)}, u32[]{:S(2)}) copy-start(f32[64]{0:T(128)S(1)} %get-tuple-element.49) | copy-start | bytes 772
  24.0 2.2 copy-start.2
  25.1 1.1 copy-start
  27.9 26.1 %all-to-all-start = ((f32[64,1,1536]{2,1,0:T(1,128)}), f32[64,1,1536]{2,1,0:T(1,128)S(1)}, u32[]{:S(2)}, u32[]{:S(2)}) async-start(f32[64,1,1536]{2,1,0:T(1,128)} %copy.144), calls=%async_computation | async-start | bytes 786432 | tf_op jit(solution)/shard_map/all_to_all | solution.py:56
  75.0 28.7 %all-to-all-start.1 = ((f32[64,1,3072]{2,1,0:T(1,128)}), f32[64,1,3072]{2,1,0:T(1,128)S(1)}, u32[]{:S(2)}, u32[]{:S(2)}) async-start(f32[64,1,3072]{2,1,0:T(1,128)} %all_to_all.57), calls=%async_computation.1 | async-start | bytes 1572864 | tf_op jit(solution)/shard_map/all_to_all | solution.py:71
  103.7 28.4 %all-to-all-start.2 = ((f32[64,1,3072]{2,1,0:T(1,128)}), f32[64,1,3072]{2,1,0:T(1,128)S(1)}, u32[]{:S(2)}, u32[]{:S(2)}) async-start(f32[64,1,3072]{2,1,0:T(1,128)} %all_to_all.58), calls=%async_computation.2 | async-start | bytes 1572864 | tf_op jit(solution)/shard_map/all_to_all | solution.py:74
  216.3 22.0 %all-to-all-start.3 = ((f32[64,1,2048]{2,1,0:T(1,128)}), f32[64,1,2048]{2,1,0:T(1,128)S(1)}, u32[]{:S(2)}, u32[]{:S(2)}) async-start(f32[64,1,2048]{2,1,0:T(1,128)} %copy.160), calls=%async_computation.3 | async-start | bytes 1048576 | tf_op jit(solution)/shard_map/all_to_all | solution.py:112
  238.3 21.5 %all-to-all-start.4 = ((f32[64,1,2048]{2,1,0:T(1,128)}), f32[64,1,2048]{2,1,0:T(1,128)S(1)}, u32[]{:S(2)}, u32[]{:S(2)}) async-start(f32[64,1,2048]{2,1,0:T(1,128)} %copy.162), calls=%async_computation.4 | async-start | bytes 1048576 | tf_op jit(solution)/shard_map/all_to_all | solution.py:113
  261.1 18.5 %copy-start.1 = (f32[64,512]{0,1:T(8,128)S(1)}, f32[64,512]{0,1:T(8,128)}, u32[]{:S(2)}) copy-start(f32[64,512]{0,1:T(8,128)} %copy-done) | copy-start | bytes 393220
  261.1 18.5 %copy-start.3 = (bf16[64,512]{0,1:T(8,128)(2,1)S(1)}, bf16[64,512]{0,1:T(8,128)(2,1)}, u32[]{:S(2)}) copy-start(bf16[64,512]{0,1:T(8,128)(2,1)} %copy-done.2) | copy-start | bytes 196612
  261.1 18.5 %copy-start.22 = (f32[64]{0:T(128)S(1)}, f32[64]{0:T(128)}, u32[]{:S(2)}) copy-start(f32[64]{0:T(128)} %param.16) | copy-start | bytes 772
  261.7 29.0 %copy-start.11 = (f32[64]{0:T(128)S(1)}, f32[64]{0:T(128)}, u32[]{:S(2)}) copy-start(f32[64]{0:T(128)} %copy-done.10) | copy-start | bytes 772
  261.8 29.0 %copy-start.13 = (f32[64]{0:T(128)S(1)}, f32[64]{0:T(128)}, u32[]{:S(2)}) copy-start(f32[64]{0:T(128)} %copy-done.12) | copy-start | bytes 772
  261.8 29.0 %copy-start.15 = (f32[64]{0:T(128)S(1)}, f32[64]{0:T(128)}, u32[]{:S(2)}) copy-start(f32[64]{0:T(128)} %copy-done.14) | copy-start | bytes 772
  262.4 29.9 %copy-start.5 = (f32[64]{0:T(128)S(1)}, f32[64]{0:T(128)}, u32[]{:S(2)}) copy-start(f32[64]{0:T(128)} %copy-done.4) | copy-start | bytes 772
  262.4 29.8 %copy-start.7 = (f32[64]{0:T(128)S(1)}, f32[64]{0:T(128)}, u32[]{:S(2)}) copy-start(f32[64]{0:T(128)} %copy-done.6) | copy-start | bytes 772
  262.4 29.8 %copy-start.9 = (f32[64]{0:T(128)S(1)}, f32[64]{0:T(128)}, u32[]{:S(2)}) copy-start(f32[64]{0:T(128)} %copy-done.8) | copy-start | bytes 772
  262.4 33.2 %copy-start.17 = (f32[64]{0:T(128)S(1)}, f32[64]{0:T(128)}, u32[]{:S(2)}) copy-start(f32[64]{0:T(128)} %copy-done.16) | copy-start | bytes 772
  262.4 33.2 %copy-start.19 = (f32[64]{0:T(128)S(1)}, f32[64]{0:T(128)}, u32[]{:S(2)}) copy-start(f32[64]{0:T(128)} %copy-done.18) | copy-start | bytes 772
  262.4 33.2 %copy-start.21 = (f32[64]{0:T(128)S(1)}, f32[64]{0:T(128)}, u32[]{:S(2)}) copy-start(f32[64]{0:T(128)} %copy-done.20) | copy-start | bytes 772
  280.9 9.9 %collective-permute-start.5 = (f32[64,2]{0,1:T(2,128)S(1)}, f32[64,2]{0,1:T(2,128)S(1)}, u32[]{:S(2)}, u32[]{:S(2)}) collective-permute-start(f32[64,2]{0,1:T(2,128)S(1)} %slice.195), channel_id=1, source_target_pairs={{4,0},{8,4},{12,8},{16,12},{20,16},{24,20},{28,24},{32,28},{36,32}... | collective-permute-start | bytes 1544 | tf_op jit(solution)/shard_map/ppermute | solution.py:12
  283.8 8.5 %collective-permute-start.4 = (f32[64,2]{0,1:T(2,128)S(1)}, f32[64,2]{0,1:T(2,128)S(1)}, u32[]{:S(2)}, u32[]{:S(2)}) collective-permute-start(f32[64,2]{0,1:T(2,128)S(1)} %slice.192), channel_id=1, source_target_pairs={{4,0},{8,4},{12,8},{16,12},{20,16},{24,20},{28,24},{32,28},{36,32}... | collective-permute-start | bytes 1544 | tf_op jit(solution)/shard_map/ppermute | solution.py:12
  287.2 8.5 %collective-permute-start.3 = (f32[64,2]{0,1:T(2,128)S(1)}, f32[64,2]{0,1:T(2,128)S(1)}, u32[]{:S(2)}, u32[]{:S(2)}) collective-permute-start(f32[64,2]{0,1:T(2,128)S(1)} %slice.188), channel_id=1, source_target_pairs={{4,0},{8,4},{12,8},{16,12},{20,16},{24,20},{28,24},{32,28},{36,32}... | collective-permute-start | bytes 1544 | tf_op jit(solution)/shard_map/ppermute | solution.py:12
where the time goes:
time: 302 us; the launch traced here: 297 us
  local copies, waits for them, and re-layouts  89 us (29%)
  starting transfers between devices  59 us (20%)
  waiting for transfers between devices  57.2 us (19%)
  other arithmetic  44.6 us (15%)
  blocking collectives  23.4 us (8%)
  matrix products  21.9 us (7%)
    add x1, other arithmetic, body(): fwd_im = filt_re * prod_im + filt_im * prod_re  22.4 us
    dot_general x20, matrix products, matmul(): return jnp.dot(left, right, precision=lax.Precision.HIGHEST)  21.9 us
    ppermute x6, starting transfers between devices, shifted(): lax.ppermute(value, axis, [(source, source + steps) for source in range(l...  19.8 us
    reshape x6, local copies, waits for them, and re-layouts, block_dft(): return (out_re.reshape(full_shape), out_im.reshape(full_shape))  19.2 us
    all_to_all x1, blocking collectives, inverse_signal(): lax.all_to_all(result_rows, 'seq', split_axis=0, concat_axis=0, tiled=True)  16.3 us
    all_to_all x1, waiting for transfers between devices, forward_spectra(): lax.all_to_all(send, 'seq', split_axis=0, concat_axis=0, tiled=True)  14.3 us
    all_to_all x1, waiting for transfers between devices, inverse_signal(): lax.all_to_all(mid_im, 'seq', split_axis=0, concat_axis=0, tiled=True)  12.9 us
    all_to_all x1, starting transfers between devices, forward_spectra(): lax.all_to_all(send, 'seq', split_axis=0, concat_axis=0, tiled=True)  11.7 us
  transfers between devices with their start and end apart: 11, of which 7 were waited for; matrix products, arithmetic and copies ran while one was open for 10% of the time, Pallas kernels for 0%

commit v1 on v0

v1 whole, which is shorter than its diff:
```python
import functools

import jax
import jax.numpy as jnp
import ml_dtypes
import numpy as np
from jax import lax
from jax.experimental import pallas as pl
from jax.experimental.pallas import tpu as pltpu
from jax.sharding import PartitionSpec as P

SEQ = 64
CHAN = 4
BLOCK = 512
LANES = 128
ROWS = 256
FILTERS = SEQ // CHAN
FULL = 2 * ROWS * LANES

BF16 = jnp.bfloat16
F32 = jnp.float32
MESH = pl.DeviceIdType.MESH


def split_table(table):
    high = table.astype(ml_dtypes.bfloat16)
    low = (table - high.astype(np.float64)).astype(ml_dtypes.bfloat16)
    return high, low


@functools.lru_cache(maxsize=None)
def tables():
    k1 = np.arange(ROWS)
    a = np.arange(ROWS)
    b = np.arange(LANES)
    outer = 2 * np.pi * ((a[None, :] * (2 * k1[:, None] + 1)) % 1024) / 1024.0
    first = np.concatenate([np.cos(outer), -np.sin(outer)], axis=0)
    last = first.T * (2.0 / FULL)
    twist = 2 * np.pi * (b[None, :] * (2 * k1[:, None] + 1)) / (2.0 * FULL)
    inner = 2 * np.pi * ((b[None, :] * b[:, None]) % LANES) / LANES
    cosine, sine = np.cos(inner), np.sin(inner)
    mid = np.block([[cosine, -sine], [sine, cosine]])
    back = np.block([[cosine, sine], [-sine, cosine]])
    first_h, first_l = split_table(first)
    last_h, last_l = split_table(last)
    mid_h, mid_l = split_table(mid)
    back_h, back_l = split_table(back)
    return (
        np.stack([first_h, first_l]),
        np.stack([last_h, last_l]),
        np.stack([mid_h, mid_l]),
        np.stack([back_h, back_l]),
        np.stack([np.cos(twist), np.sin(twist)]).astype(np.float32),
    )


def split(value):
    high = value.astype(BF16)
    low = (value - high.astype(F32)).astype(BF16)
    return high, low


def dot(left, right):
    return jnp.dot(left, right, preferred_element_type=F32)


def table_left(table, high, low):
    table_h, table_l = table[0], table[1]
    left = jnp.concatenate([table_h, table_h, table_l], axis=1)
    return dot(left, jnp.concatenate([high, low, high], axis=0))


def table_right(high, low, table):
    table_h, table_l = table[0], table[1]
    right = jnp.concatenate([table_h, table_h, table_l], axis=0)
    return dot(jnp.concatenate([high, low, high], axis=1), right)


def swap_matrix():
    row = lax.broadcasted_iota(jnp.int32, (256, 256), 0)
    col = lax.broadcasted_iota(jnp.int32, (256, 256), 1)
    hit = (row % 16 == col // 16) & (row // 16 == col % 16)
    return jnp.where(hit, 1.0, 0.0).astype(BF16)


def sort_matrix(outer, kinds, to_kinds):
    size = outer * kinds * 4
    row = lax.broadcasted_iota(jnp.int32, (size, size), 0)
    col = lax.broadcasted_iota(jnp.int32, (size, size), 1)
    by_kind, by_shard = (row, col) if to_kinds else (col, row)
    kind = by_kind // (outer * 4)
    shard = (by_kind // 4) % outer
    hit = by_shard == shard * (kinds * 4) + kind * 4 + by_kind % 4
    return jnp.where(hit, 1.0, 0.0).astype(BF16)


def delayed(value, steps):
    lane = lax.broadcasted_iota(jnp.int32, (ROWS, LANES), 1)
    row = lax.broadcasted_iota(jnp.int32, (ROWS, LANES), 0)
    turned = pltpu.roll(value, steps, 1)
    above = jnp.where(row == 0, 0.0, pltpu.roll(turned, 1, 0))
    return jnp.where(lane < steps, above, turned)


def advanced(value, steps):
    lane = lax.broadcasted_iota(jnp.int32, (ROWS, LANES), 1)
    row = lax.broadcasted_iota(jnp.int32, (ROWS, LANES), 0)
    turned = pltpu.roll(value, LANES - steps, 1)
    below = jnp.where(row == ROWS - 1, 0.0, pltpu.roll(turned, ROWS - 1, 0))
    return jnp.where(lane >= LANES - steps, below, turned)


def kernel(
    q_ref, k_ref, v_ref, g_ref, filt_ref, qt_ref, kt_ref, vt_ref, gain_ref,
    first_hbm, last_hbm, mid_hbm, back_hbm, twist_hbm,
    oq_ref, dq_ref, dk_ref, dv_ref,
    first_ref, last_ref, mid_ref, back_ref, twist_ref,
    send_x, recv_x, send_f, recv_f, send_y, recv_y,
    table_sem, send_x_sem, recv_x_sem, send_f_sem, recv_f_sem,
    share_send_sem, share_recv_sem, send_y_sem, recv_y_sem,
):
    me = lax.axis_index("seq")
    group = lax.axis_index("chan")
    me_z, me_x, me_y = me // 8, (me // 2) % 4, me % 2

    def partner(step):
        dz = (step * 3) % 8
        dx = (step // 8) % 4
        dy = step // 32
        return ((me_z + dz) % 8) * 8 + ((me_x + dx) % 4) * 2 + (me_y + dy) % 2

    table_copies = [
        pltpu.make_async_copy(source, target, table_sem.at[index])
        for index, (source, target) in enumerate(
            [
                (first_hbm, first_ref),
                (mid_hbm, mid_ref),
                (twist_hbm, twist_ref),
                (back_hbm, back_ref),
                (last_hbm, last_ref),
            ]
        )
    ]

    barrier = pltpu.get_barrier_semaphore()

    def greet(step, carry):
        pl.semaphore_signal(barrier, inc=1, device_id={"seq": partner(step)}, device_id_type=MESH)
        return carry

    lax.fori_loop(1, SEQ, greet, 0)
    source_group = me // FILTERS

    def greet_source(step, carry):
        source = group * FILTERS + (me + step) % FILTERS

        @pl.when(jnp.logical_not((source == me) & (source_group == group)))
        def _():
            pl.semaphore_signal(
                barrier, inc=1, device_id={"seq": source, "chan": source_group}, device_id_type=MESH
            )

        return carry

    lax.fori_loop(0, FILTERS, greet_source, 0)
    for step in range(1, CHAN):
        pl.semaphore_signal(
            barrier, inc=1, device_id={"chan": (group + step) % CHAN}, device_id_type=MESH
        )
    for copy in table_copies:
        copy.start()

    filt_h, filt_l = split(filt_ref[...])
    pieces = [part[:, LANES * j : LANES * (j + 1)] for part in (filt_h, filt_l) for j in range(4)]
    row = lax.broadcasted_iota(jnp.int32, (128, 128), 0)
    col = lax.broadcasted_iota(jnp.int32, (128, 128), 1)
    regroup = jnp.where((row % 8 == col // 16) & (row // 8 == col % 16), 1.0, 0.0).astype(BF16)
    send_f[...] = dot(regroup, jnp.concatenate(pieces, axis=0)).astype(BF16).reshape(FILTERS, 8, LANES)
    swap = swap_matrix()
    for m in range(4):
        pieces = [
            ref[16 * m : 16 * (m + 1), LANES * j : LANES * (j + 1)]
            for ref in (q_ref, k_ref, v_ref, g_ref)
            for j in range(4)
        ]
        mixed_rows = dot(swap, jnp.concatenate(pieces, axis=0)).astype(BF16)
        send_x[16 * m : 16 * (m + 1)] = mixed_rows.reshape(16, 16, LANES)

    own_filter = (me // FILTERS == group) & (source_group == group)
    pl.semaphore_wait(barrier, SEQ - 1 + FILTERS + CHAN - 1 - own_filter.astype(jnp.int32))

    def send_filter(step, carry):
        r = (me + step) % FILTERS
        target = group * FILTERS + r
        to_self = (target == me) & (source_group == group)

        @pl.when(to_self)
        def _():
            pltpu.make_async_copy(send_f.at[r], recv_f.at[me], recv_f_sem).start()

        @pl.when(jnp.logical_not(to_self))
        def _():
            pltpu.make_async_remote_copy(
                src_ref=send_f.at[r],
                dst_ref=recv_f.at[me],
                send_sem=send_f_sem,
                recv_sem=recv_f_sem,
                device_id={"seq": target, "chan": source_group},
                device_id_type=MESH,
            ).start()

        return carry

    lax.fori_loop(0, FILTERS, send_filter, 0)

    pltpu.make_async_copy(send_x.at[me], recv_x.at[me], recv_x_sem).start()

    def send_inputs(step, carry):
        target = partner(step)
        pltpu.make_async_remote_copy(
            src_ref=send_x.at[target],
            dst_ref=recv_x.at[me],
            send_sem=send_x_sem,
            recv_sem=recv_x_sem,
            device_id={"seq": target},
            device_id_type=MESH,
        ).start()
        return carry

    lax.fori_loop(1, SEQ, send_inputs, 0)

    part = recv_f.at[pl.ds(group * FILTERS, FILTERS)]
    pltpu.make_async_copy(part, part, recv_f_sem).wait()
    for step in range(1, CHAN):
        pltpu.make_async_remote_copy(
            src_ref=part,
            dst_ref=part,
            send_sem=share_send_sem,
            recv_sem=share_recv_sem,
            device_id={"chan": (group + step) % CHAN},
            device_id_type=MESH,
        ).start()
    three = recv_f.at[pl.ds(0, (CHAN - 1) * FILTERS)]
    pltpu.make_async_copy(three, three, share_recv_sem).wait()

    sort_f = sort_matrix(32, 2, True)
    filt_hi, filt_lo = [], []
    for m in range(2):
        got = recv_f[32 * m : 32 * (m + 1)].reshape(256, LANES)
        rows = dot(sort_f, got).astype(BF16)
        filt_hi.append(rows[:128])
        filt_lo.append(rows[128:])

    for copy in table_copies:
        copy.wait()

    pltpu.make_async_copy(recv_x, recv_x, recv_x_sem).wait()
    sort_x = sort_matrix(16, 4, True)
    parts = []
    for m in range(4):
        got = recv_x[16 * m : 16 * (m + 1)].reshape(256, LANES)
        parts.append(dot(sort_x, got))
    query, key, value, cotangent = (
        jnp.concatenate([rows[64 * i : 64 * (i + 1)] for rows in parts], axis=0) for i in range(4)
    )

    def causal_taps(signal, taps):
        return (
            taps[0, me] * signal + taps[1, me] * delayed(signal, 1) + taps[2, me] * delayed(signal, 2)
        )

    def reverse_taps(signal, taps):
        return (
            taps[0, me] * signal + taps[1, me] * advanced(signal, 1) + taps[2, me] * advanced(signal, 2)
        )

    short_q = causal_taps(query, qt_ref)
    short_k = causal_taps(key, kt_ref)
    short_v = causal_taps(value, vt_ref)
    product = short_k * short_v
    grad_mixed = cotangent * short_q

    prod_h, prod_l = split(product)
    grad_h, grad_l = split(grad_mixed)
    high = jnp.concatenate([jnp.concatenate(filt_hi, axis=0), prod_h, grad_h], axis=1)
    low = jnp.concatenate([jnp.concatenate(filt_lo, axis=0), prod_l, grad_l], axis=1)
    outer = table_left(first_ref, high, low)
    cosine, sine = twist_ref[0], twist_ref[1]

    def spectrum(index):
        real = outer[:ROWS, LANES * index : LANES * (index + 1)]
        imag = outer[ROWS:, LANES * index : LANES * (index + 1)]
        turned = jnp.concatenate([real * cosine + imag * sine, imag * cosine - real * sine], axis=1)
        whole = table_right(*split(turned), mid_ref)
        return whole[:, :LANES], whole[:, LANES:]

    filt_re, filt_im = spectrum(0)

    def inverse(real, imag):
        back = table_right(*split(jnp.concatenate([real, imag], axis=1)), back_ref)
        real, imag = back[:, :LANES], back[:, LANES:]
        return jnp.concatenate([real * cosine - imag * sine, imag * cosine + real * sine], axis=0)

    prod_re, prod_im = spectrum(1)
    fwd = inverse(filt_re * prod_re - filt_im * prod_im, filt_re * prod_im + filt_im * prod_re)
    grad_re, grad_im = spectrum(2)
    bwd = inverse(filt_re * grad_re + filt_im * grad_im, filt_re * grad_im - filt_im * grad_re)
    both = table_left(last_ref, *split(jnp.concatenate([fwd, bwd], axis=1)))
    causal, backward = both[:, :LANES], both[:, LANES:]

    gain = gain_ref[me]
    mixed = causal + gain * product
    gated = short_q * mixed
    grad_product = backward + gain * grad_mixed
    outs = [
        gated.astype(BF16),
        reverse_taps(cotangent * mixed, qt_ref).astype(BF16),
        reverse_taps(grad_product * short_v, kt_ref).astype(BF16),
        reverse_taps(grad_product * short_k, vt_ref).astype(BF16),
    ]
    sort_y = sort_matrix(16, 4, False)
    for m in range(4):
        rows = jnp.concatenate([out[64 * m : 64 * (m + 1)] for out in outs], axis=0)
        send_y[16 * m : 16 * (m + 1)] = dot(sort_y, rows).astype(BF16).reshape(16, 16, LANES)

    pltpu.make_async_copy(send_y.at[me], recv_y.at[me], recv_y_sem).start()

    def send_outputs(step, carry):
        target = partner(step)
        pltpu.make_async_remote_copy(
            src_ref=send_y.at[target],
            dst_ref=recv_y.at[me],
            send_sem=send_y_sem,
            recv_sem=recv_y_sem,
            device_id={"seq": target},
            device_id_type=MESH,
        ).start()
        return carry

    lax.fori_loop(1, SEQ, send_outputs, 0)

    sent = send_x.at[pl.ds(0, SEQ - 1)]
    pltpu.make_async_copy(sent, sent, send_x_sem).wait()
    pltpu.make_async_copy(three, three, share_send_sem).wait()

    @pl.when(own_filter)
    def _():
        some = send_f.at[pl.ds(0, FILTERS - 1)]
        pltpu.make_async_copy(some, some, send_f_sem).wait()

    @pl.when(jnp.logical_not(own_filter))
    def _():
        pltpu.make_async_copy(send_f, send_f, send_f_sem).wait()

    pltpu.make_async_copy(recv_y, recv_y, recv_y_sem).wait()
    for m in range(4):
        rows = dot(swap, recv_y[16 * m : 16 * (m + 1)].reshape(256, LANES)).astype(BF16)
        for i, ref in enumerate((oq_ref, dq_ref, dk_ref, dv_ref)):
            for j in range(4):
                at = (4 * i + j) * 16
                ref[16 * m : 16 * (m + 1), LANES * j : LANES * (j + 1)] = rows[at : at + 16]
    sent = send_y.at[pl.ds(0, SEQ - 1)]
    pltpu.make_async_copy(sent, sent, send_y_sem).wait()


def body(q, k, v, long_filter, q_taps, k_taps, v_taps, gain, cotangent):
    constants = [jnp.asarray(table) for table in tables()]
    vmem = pl.BlockSpec(memory_space=pltpu.VMEM)
    smem = pl.BlockSpec(memory_space=pltpu.SMEM)
    anywhere = pl.BlockSpec(memory_space=pl.ANY)
    block = jax.ShapeDtypeStruct((SEQ, BLOCK), BF16)
    exchange = pltpu.VMEM((SEQ, 16, LANES), BF16)
    return pl.pallas_call(
        kernel,
        out_shape=[block] * 4,
        in_specs=[vmem] * 5 + [smem] * 4 + [anywhere] * 5,
        out_specs=[vmem] * 4,
        scratch_shapes=[
            pltpu.VMEM((2, 512, 256), BF16),
            pltpu.VMEM((2, 256, 512), BF16),
            pltpu.VMEM((2, 256, 256), BF16),
            pltpu.VMEM((2, 256, 256), BF16),
            pltpu.VMEM((2, ROWS, LANES), F32),
            exchange,
            exchange,
            pltpu.VMEM((FILTERS, 8, LANES), BF16),
            pltpu.VMEM((SEQ, 8, LANES), BF16),
            exchange,
            exchange,
            pltpu.SemaphoreType.DMA((5,)),
        ]
        + [pltpu.SemaphoreType.DMA] * 8,
        compiler_params=pltpu.CompilerParams(
            collective_id=0, has_side_effects=True, vmem_limit_bytes=40 * 1024 * 1024
        ),
        name="hyena",
    )(q, k, v, cotangent, long_filter, q_taps, k_taps, v_taps, gain, *constants)


def solution(mesh):
    in_specs = (
        P("chan", "seq"),
        P("chan", "seq"),
        P("chan", "seq"),
        P("chan", "seq"),
        P(None, "chan"),
        P(None, "chan"),
        P(None, "chan"),
        P("chan"),
        P("chan", "seq"),
    )
    out_specs = (P("chan", "seq"),) * 4
    return jax.shard_map(body, mesh=mesh, in_specs=in_specs, out_specs=out_specs, check_vma=False)
```

time: 302 us -> 53.9 us (0.18)
  the two profiles are of different devices: /device:TPU:30 before, /device:TPU:16 now
where the time goes in v1:
time: 53.9 us; the launch traced here: 53.3 us
  Pallas kernels  38.4 us (71%)
  local copies, waits for them, and re-layouts  14.3 us (27%)
  between operations  0.67 us (1%)
    pallas_call x1, Pallas kernels, body(): pl.pallas_call(kernel, out_shape=[block] * 4, in_specs=[vmem] * 5 + [smem...  38.4 us
    unnamed x32, local copies, waits for them, and re-layouts  14.3 us

profile of v1, /device:TPU:16, one launch (start us, length us, event | category | flops | bytes accessed | tf_op | source)
XLA Modules:
  0.0 53.3 jit_solution(12457346035233210837)
XLA Ops:
  0.6 0.0 copy-start
  0.6 1.0 %copy-done = bf16[2,256,512]{2,1,0:T(8,128)(2,1)S(1)} copy-done((bf16[2,256,512]{2,1,0:T(8,128)(2,1)S(1)}, bf16[2,256,512]{2,1,0:T(8,128)(2,1)}, u32[]{:S(2)}) %copy-start) | copy-done | bytes 524312
  1.7 0.0 copy-start.1
  1.7 1.0 %copy-done.1 = bf16[2,512,256]{2,1,0:T(8,128)(2,1)S(1)} copy-done((bf16[2,512,256]{2,1,0:T(8,128)(2,1)S(1)}, bf16[2,512,256]{2,1,0:T(8,128)(2,1)}, u32[]{:S(2)}) %copy-start.1) | copy-done | bytes 524312
  2.7 0.0 copy-start.2
  2.7 0.9 %copy-done.2 = f32[2,256,128]{2,1,0:T(8,128)S(1)} copy-done((f32[2,256,128]{2,1,0:T(8,128)S(1)}, f32[2,256,128]{2,1,0:T(8,128)}, u32[]{:S(2)}) %copy-start.2) | copy-done | bytes 262168
  3.7 0.0 copy-start.3
  3.7 0.9 %copy-done.3 = bf16[2,256,256]{2,1,0:T(8,128)(2,1)S(1)} copy-done((bf16[2,256,256]{2,1,0:T(8,128)(2,1)S(1)}, bf16[2,256,256]{2,1,0:T(8,128)(2,1)}, u32[]{:S(2)}) %copy-start.3) | copy-done | bytes 262168
  4.6 0.0 copy-start.4
  4.6 0.9 %copy-done.4 = bf16[2,256,256]{2,1,0:T(8,128)(2,1)S(1)} copy-done((bf16[2,256,256]{2,1,0:T(8,128)(2,1)S(1)}, bf16[2,256,256]{2,1,0:T(8,128)(2,1)}, u32[]{:S(2)}) %copy-start.4) | copy-done | bytes 262168
  5.6 0.0 copy-start.5
  5.6 0.8 %copy-done.5 = bf16[64,512]{1,0:T(8,128)(2,1)S(1)} copy-done((bf16[64,512]{1,0:T(8,128)(2,1)S(1)}, bf16[64,512]{1,0:T(8,128)(2,1)}, u32[]{:S(2)}) %copy-start.5) | copy-done | bytes 65560
  6.4 0.0 copy-start.6
  6.4 0.8 %copy-done.6 = bf16[64,512]{1,0:T(8,128)(2,1)S(1)} copy-done((bf16[64,512]{1,0:T(8,128)(2,1)S(1)}, bf16[64,512]{1,0:T(8,128)(2,1)}, u32[]{:S(2)}) %copy-start.6) | copy-done | bytes 65560
  7.3 0.0 copy-start.7
  7.3 0.8 %copy-done.7 = bf16[64,512]{1,0:T(8,128)(2,1)S(1)} copy-done((bf16[64,512]{1,0:T(8,128)(2,1)S(1)}, bf16[64,512]{1,0:T(8,128)(2,1)}, u32[]{:S(2)}) %copy-start.7) | copy-done | bytes 65560
  8.1 0.0 copy-start.8
  8.1 0.8 %copy-done.8 = bf16[64,512]{1,0:T(8,128)(2,1)S(1)} copy-done((bf16[64,512]{1,0:T(8,128)(2,1)S(1)}, bf16[64,512]{1,0:T(8,128)(2,1)}, u32[]{:S(2)}) %copy-start.8) | copy-done | bytes 65560
  8.9 0.0 copy-start.9
  8.9 0.8 %copy-done.9 = f32[16,512]{1,0:T(8,128)S(1)} copy-done((f32[16,512]{1,0:T(8,128)S(1)}, f32[16,512]{1,0:T(8,128)}, u32[]{:S(2)}) %copy-start.9) | copy-done | bytes 32792
  9.7 0.0 copy-start.10
  9.7 0.7 %copy-done.10 = f32[3,64]{1,0:T(4,128)S(1)} copy-done((f32[3,64]{1,0:T(4,128)S(1)}, f32[3,64]{1,0:T(4,128)}, u32[]{:S(2)}) %copy-start.10) | copy-done | bytes 792
  10.4 0.0 copy-start.11
  10.4 0.7 %copy-done.11 = f32[3,64]{1,0:T(4,128)S(1)} copy-done((f32[3,64]{1,0:T(4,128)S(1)}, f32[3,64]{1,0:T(4,128)}, u32[]{:S(2)}) %copy-start.11) | copy-done | bytes 792
  11.1 0.0 copy-start.12
  11.1 0.7 %copy-done.12 = f32[3,64]{1,0:T(4,128)S(1)} copy-done((f32[3,64]{1,0:T(4,128)S(1)}, f32[3,64]{1,0:T(4,128)}, u32[]{:S(2)}) %copy-start.12) | copy-done | bytes 792
  11.7 0.0 copy-start.13
  11.7 0.7 %copy-done.13 = f32[64]{0:T(128)S(1)} copy-done((f32[64]{0:T(128)S(1)}, f32[64]{0:T(128)}, u32[]{:S(2)}) %copy-start.13) | copy-done | bytes 280
  12.4 38.4 %hyena.1 = (bf16[64,512]{1,0:T(8,128)(2,1)S(1)}, bf16[64,512]{1,0:T(8,128)(2,1)S(1)}, bf16[64,512]{1,0:T(8,128)(2,1)S(1)}, bf16[64,512]{1,0:T(8,128)(2,1)S(1)}) custom-call(bf16[64,512]{1,0:T(8,128)(2,1)S(1)} %copy-done.5, bf16[64,512]{1,0:T(8,128)(2,1)S(1)} %copy-done.6, bf16[64,512]{1,0:T(8,128)(2,1)S(1)} %copy-done.7, bf16[64,512]{1,0:T(8,128)(2,1)S(1)} %copy-done.8, ...), custom_call_target="tpu_custom_call" | custom-call | tf_op jit(solution)/shard_map/hyena/pallas_call | solution.py:373
  50.8 0.6 %copy.22 = bf16[64,512]{1,0:T(8,128)(2,1)} copy(bf16[64,512]{1,0:T(8,128)(2,1)S(1)} %get-tuple-element.8) | data formatting | bytes 131072
  51.4 0.6 %copy.23 = bf16[64,512]{1,0:T(8,128)(2,1)} copy(bf16[64,512]{1,0:T(8,128)(2,1)S(1)} %get-tuple-element.9) | data formatting | bytes 131072
  52.1 0.6 %copy.24 = bf16[64,512]{1,0:T(8,128)(2,1)} copy(bf16[64,512]{1,0:T(8,128)(2,1)S(1)} %get-tuple-element.10) | data formatting | bytes 131072
  52.7 0.6 %copy.25 = bf16[64,512]{1,0:T(8,128)(2,1)} copy(bf16[64,512]{1,0:T(8,128)(2,1)S(1)} %get-tuple-element.11) | data formatting | bytes 131072
Async XLA Ops:
  0.6 1.0 %copy-start = (bf16[2,256,512]{2,1,0:T(8,128)(2,1)S(1)}, bf16[2,256,512]{2,1,0:T(8,128)(2,1)}, u32[]{:S(2)}) copy-start(bf16[2,256,512]{2,1,0:T(8,128)(2,1)} %constant.11.clone.last_hbm) | copy-start | bytes 1572868
  1.7 1.0 %copy-start.1 = (bf16[2,512,256]{2,1,0:T(8,128)(2,1)S(1)}, bf16[2,512,256]{2,1,0:T(8,128)(2,1)}, u32[]{:S(2)}) copy-start(bf16[2,512,256]{2,1,0:T(8,128)(2,1)} %constant.10.clone.first_hbm) | copy-start | bytes 1572868
  2.7 0.9 %copy-start.2 = (f32[2,256,128]{2,1,0:T(8,128)S(1)}, f32[2,256,128]{2,1,0:T(8,128)}, u32[]{:S(2)}) copy-start(f32[2,256,128]{2,1,0:T(8,128)} %constant.14.clone.twist_hbm) | copy-start | bytes 786436
  3.7 0.9 %copy-start.3 = (bf16[2,256,256]{2,1,0:T(8,128)(2,1)S(1)}, bf16[2,256,256]{2,1,0:T(8,128)(2,1)}, u32[]{:S(2)}) copy-start(bf16[2,256,256]{2,1,0:T(8,128)(2,1)} %constant.13.clone.back_hbm) | copy-start | bytes 786436
  4.6 0.9 %copy-start.4 = (bf16[2,256,256]{2,1,0:T(8,128)(2,1)S(1)}, bf16[2,256,256]{2,1,0:T(8,128)(2,1)}, u32[]{:S(2)}) copy-start(bf16[2,256,256]{2,1,0:T(8,128)(2,1)} %constant.12.clone.mid_hbm) | copy-start | bytes 786436
  5.6 0.8 %copy-start.5 = (bf16[64,512]{1,0:T(8,128)(2,1)S(1)}, bf16[64,512]{1,0:T(8,128)(2,1)}, u32[]{:S(2)}) copy-start(bf16[64,512]{1,0:T(8,128)(2,1)} %q_ref.1) | copy-start | bytes 196612
  6.4 0.8 %copy-start.6 = (bf16[64,512]{1,0:T(8,128)(2,1)S(1)}, bf16[64,512]{1,0:T(8,128)(2,1)}, u32[]{:S(2)}) copy-start(bf16[64,512]{1,0:T(8,128)(2,1)} %k_ref.1) | copy-start | bytes 196612
  7.3 0.8 %copy-start.7 = (bf16[64,512]{1,0:T(8,128)(2,1)S(1)}, bf16[64,512]{1,0:T(8,128)(2,1)}, u32[]{:S(2)}) copy-start(bf16[64,512]{1,0:T(8,128)(2,1)} %v_ref.1) | copy-start | bytes 196612
  8.1 0.8 %copy-start.8 = (bf16[64,512]{1,0:T(8,128)(2,1)S(1)}, bf16[64,512]{1,0:T(8,128)(2,1)}, u32[]{:S(2)}) copy-start(bf16[64,512]{1,0:T(8,128)(2,1)} %g_ref.1) | copy-start | bytes 196612
  8.9 0.8 %copy-start.9 = (f32[16,512]{1,0:T(8,128)S(1)}, f32[16,512]{1,0:T(8,128)}, u32[]{:S(2)}) copy-start(f32[16,512]{1,0:T(8,128)} %filt_ref.1) | copy-start | bytes 98308
  9.7 0.7 %copy-start.10 = (f32[3,64]{1,0:T(4,128)S(1)}, f32[3,64]{1,0:T(4,128)}, u32[]{:S(2)}) copy-start(f32[3,64]{1,0:T(4,128)} %qt_ref.1) | copy-start | bytes 2308
  10.4 0.7 %copy-start.11 = (f32[3,64]{1,0:T(4,128)S(1)}, f32[3,64]{1,0:T(4,128)}, u32[]{:S(2)}) copy-start(f32[3,64]{1,0:T(4,128)} %kt_ref.1) | copy-start | bytes 2308
  11.1 0.7 %copy-start.12 = (f32[3,64]{1,0:T(4,128)S(1)}, f32[3,64]{1,0:T(4,128)}, u32[]{:S(2)}) copy-start(f32[3,64]{1,0:T(4,128)} %vt_ref.1) | copy-start | bytes 2308
  11.7 0.7 %copy-start.13 = (f32[64]{0:T(128)S(1)}, f32[64]{0:T(128)}, u32[]{:S(2)}) copy-start(f32[64]{0:T(128)} %gain_ref.1) | copy-start | bytes 772

commit v2 on v1

--- a/solution.py
+++ b/solution.py
@@ -16,6 +16,7 @@
 ROWS = 256
 FILTERS = SEQ // CHAN
 FULL = 2 * ROWS * LANES
+VMEM_LIMIT = 60 * 1024 * 1024
 
 BF16 = jnp.bfloat16
 F32 = jnp.float32
@@ -111,12 +112,13 @@
 
 
 def kernel(
+    q_hbm, k_hbm, v_hbm, g_hbm, filt_hbm, qt_hbm, kt_hbm, vt_hbm, gain_hbm,
+    first_hbm, last_hbm, mid_hbm, back_hbm, twist_hbm,
+    out_hbm,
     q_ref, k_ref, v_ref, g_ref, filt_ref, qt_ref, kt_ref, vt_ref, gain_ref,
-    first_hbm, last_hbm, mid_hbm, back_hbm, twist_hbm,
-    oq_ref, dq_ref, dk_ref, dv_ref,
     first_ref, last_ref, mid_ref, back_ref, twist_ref,
     send_x, recv_x, send_f, recv_f, send_y, recv_y,
-    table_sem, send_x_sem, recv_x_sem, send_f_sem, recv_f_sem,
+    input_sem, taps_sem, table_sem, out_sem, send_x_sem, recv_x_sem, send_f_sem, recv_f_sem,
     share_send_sem, share_recv_sem, send_y_sem, recv_y_sem,
 ):
     me = lax.axis_index("seq")
@@ -129,18 +131,31 @@
         dy = step // 32
         return ((me_z + dz) % 8) * 8 + ((me_x + dx) % 4) * 2 + (me_y + dy) % 2
 
-    table_copies = [
-        pltpu.make_async_copy(source, target, table_sem.at[index])
-        for index, (source, target) in enumerate(
-            [
-                (first_hbm, first_ref),
-                (mid_hbm, mid_ref),
-                (twist_hbm, twist_ref),
-                (back_hbm, back_ref),
-                (last_hbm, last_ref),
-            ]
-        )
-    ]
+    def copies(pairs, sems):
+        return [
+            pltpu.make_async_copy(source, target, sems.at[index])
+            for index, (source, target) in enumerate(pairs)
+        ]
+
+    input_copies = copies(
+        [(filt_hbm, filt_ref), (q_hbm, q_ref), (k_hbm, k_ref), (v_hbm, v_ref), (g_hbm, g_ref)],
+        input_sem,
+    )
+    taps_copies = copies(
+        [(qt_hbm, qt_ref), (kt_hbm, kt_ref), (vt_hbm, vt_ref), (gain_hbm, gain_ref)], taps_sem
+    )
+    table_copies = copies(
+        [
+            (first_hbm, first_ref),
+            (mid_hbm, mid_ref),
+            (twist_hbm, twist_ref),
+            (back_hbm, back_ref),
+            (last_hbm, last_ref),
+        ],
+        table_sem,
+    )
+    for copy in input_copies:
+        copy.start()
 
     barrier = pltpu.get_barrier_semaphore()
 
@@ -167,8 +182,10 @@
         pl.semaphore_signal(
             barrier, inc=1, device_id={"chan": (group + step) % CHAN}, device_id_type=MESH
         )
-    for copy in table_copies:
+    for copy in taps_copies + table_copies:
         copy.start()
+    for copy in input_copies:
+        copy.wait()
 
     filt_h, filt_l = split(filt_ref[...])
     pieces = [part[:, LANES * j : LANES * (j + 1)] for part in (filt_h, filt_l) for j in range(4)]
@@ -251,7 +268,7 @@
         filt_hi.append(rows[:128])
         filt_lo.append(rows[128:])
 
-    for copy in table_copies:
+    for copy in taps_copies + table_copies:
         copy.wait()
 
     pltpu.make_async_copy(recv_x, recv_x, recv_x_sem).wait()
@@ -353,29 +370,50 @@
         pltpu.make_async_copy(send_f, send_f, send_f_sem).wait()
 
     pltpu.make_async_copy(recv_y, recv_y, recv_y_sem).wait()
+    result = pltpu.make_async_copy(recv_y, out_hbm, out_sem)
+    result.start()
+    sent = send_y.at[pl.ds(0, SEQ - 1)]
+    pltpu.make_async_copy(sent, sent, send_y_sem).wait()
+    result.wait()
+
+
+def scatter_kernel(in_hbm, *refs):
+    out_hbm, (in_ref, *out_refs), (in_sem, out_sem) = refs[:4], refs[4:9], refs[9:]
+    copy = pltpu.make_async_copy(in_hbm, in_ref, in_sem)
+    copy.start()
+    swap = swap_matrix()
+    copy.wait()
     for m in range(4):
-        rows = dot(swap, recv_y[16 * m : 16 * (m + 1)].reshape(256, LANES)).astype(BF16)
-        for i, ref in enumerate((oq_ref, dq_ref, dk_ref, dv_ref)):
+        rows = dot(swap, in_ref[16 * m : 16 * (m + 1)].reshape(256, LANES)).astype(BF16)
+        for i, ref in enumerate(out_refs):
             for j in range(4):
                 at = (4 * i + j) * 16
                 ref[16 * m : 16 * (m + 1), LANES * j : LANES * (j + 1)] = rows[at : at + 16]
-    sent = send_y.at[pl.ds(0, SEQ - 1)]
-    pltpu.make_async_copy(sent, sent, send_y_sem).wait()
+    stores = [
+        pltpu.make_async_copy(ref, hbm, out_sem.at[i])
+        for i, (ref, hbm) in enumerate(zip(out_refs, out_hbm))
+    ]
+    for store in stores:
+        store.start()
+    for store in stores:
+        store.wait()
 
 
 def body(q, k, v, long_filter, q_taps, k_taps, v_taps, gain, cotangent):
     constants = [jnp.asarray(table) for table in tables()]
-    vmem = pl.BlockSpec(memory_space=pltpu.VMEM)
-    smem = pl.BlockSpec(memory_space=pltpu.SMEM)
     anywhere = pl.BlockSpec(memory_space=pl.ANY)
-    block = jax.ShapeDtypeStruct((SEQ, BLOCK), BF16)
+    block = pltpu.VMEM((SEQ, BLOCK), BF16)
     exchange = pltpu.VMEM((SEQ, 16, LANES), BF16)
-    return pl.pallas_call(
+    arrived = pl.pallas_call(
         kernel,
-        out_shape=[block] * 4,
-        in_specs=[vmem] * 5 + [smem] * 4 + [anywhere] * 5,
-        out_specs=[vmem] * 4,
-        scratch_shapes=[
+        out_shape=jax.ShapeDtypeStruct((SEQ, 16, LANES), BF16),
+        in_specs=[anywhere] * 14,
+        out_specs=anywhere,
+        scratch_shapes=[block] * 4
+        + [pltpu.VMEM((FILTERS, BLOCK), F32)]
+        + [pltpu.SMEM((3, SEQ), F32)] * 3
+        + [pltpu.SMEM((SEQ,), F32)]
+        + [
             pltpu.VMEM((2, 512, 256), BF16),
             pltpu.VMEM((2, 256, 512), BF16),
             pltpu.VMEM((2, 256, 256), BF16),
@@ -388,13 +426,24 @@
             exchange,
             exchange,
             pltpu.SemaphoreType.DMA((5,)),
+            pltpu.SemaphoreType.DMA((4,)),
+            pltpu.SemaphoreType.DMA((5,)),
         ]
-        + [pltpu.SemaphoreType.DMA] * 8,
+        + [pltpu.SemaphoreType.DMA] * 9,
         compiler_params=pltpu.CompilerParams(
-            collective_id=0, has_side_effects=True, vmem_limit_bytes=40 * 1024 * 1024
+            collective_id=0, has_side_effects=True, vmem_limit_bytes=VMEM_LIMIT
         ),
         name="hyena",
     )(q, k, v, cotangent, long_filter, q_taps, k_taps, v_taps, gain, *constants)
+    return pl.pallas_call(
+        scatter_kernel,
+        out_shape=[jax.ShapeDtypeStruct((SEQ, BLOCK), BF16)] * 4,
+        in_specs=[anywhere],
+        out_specs=[anywhere] * 4,
+        scratch_shapes=[exchange] + [block] * 4 + [pltpu.SemaphoreType.DMA, pltpu.SemaphoreType.DMA((4,))],
+        compiler_params=pltpu.CompilerParams(vmem_limit_bytes=VMEM_LIMIT),
+        name="scatter_rows",
+    )(arrived)
 
 
 def solution(mesh):

time: 53.9 us -> 41.1 us (0.76)
  local copies, waits for them, and re-layouts: 14.3 us -> 0 us
  Pallas kernels: 38.4 us -> 40.4 us
    unnamed x32 -> x0, local copies, waits for them, and re-layouts: 14.3 us -> none
    pallas_call x1 -> x2, Pallas kernels: 38.4 us -> 40.4 us  [the longest x1 38.4 us: body(): pl.pallas_call(kernel, out_shape=jax.ShapeDtypeStruct((SEQ, 16, LANES), B...]
where the time goes in v2:
time: 41.1 us; the launch traced here: 41 us
  Pallas kernels  40.4 us (98%)
  between operations  0.64 us (2%)
    pallas_call x1, Pallas kernels, body(): pl.pallas_call(kernel, out_shape=jax.ShapeDtypeStruct((SEQ, 16, LANES), B...  38.4 us
    pallas_call x1, Pallas kernels, body(): pl.pallas_call(scatter_kernel, out_shape=[jax.ShapeDtypeStruct((SEQ, BLOC...  1.92 us

profile of v2, /device:TPU:16, one launch (start us, length us, event | category | flops | bytes accessed | tf_op | source)
XLA Modules:
  0.0 41.0 jit_solution(730652005155820756)
XLA Ops:
  0.6 38.4 %hyena.1.in_hbm = bf16[64,16,128]{2,1,0:T(8,128)(2,1)} custom-call(bf16[64,512]{1,0:T(8,128)(2,1)} %q_hbm.1, bf16[64,512]{1,0:T(8,128)(2,1)} %k_hbm.1, bf16[64,512]{1,0:T(8,128)(2,1)} %v_hbm.1, bf16[64,512]{1,0:T(8,128)(2,1)} %g_hbm.1, f32[16,512]{1,0:T(8,128)} %filt_hbm.1, f32[3,64]{1,0:T(4,128)} %qt_hbm.1, f32[3,64]{1,0:T(4,128)} %kt_hbm.1, ...), custom_call_target="tpu_custom_call" | custom-call | tf_op jit(solution)/shard_map/hyena/pallas_call | solution.py:407
  39.1 1.9 %scatter_rows.1 = (bf16[64,512]{1,0:T(8,128)(2,1)}, bf16[64,512]{1,0:T(8,128)(2,1)}, bf16[64,512]{1,0:T(8,128)(2,1)}, bf16[64,512]{1,0:T(8,128)(2,1)}) custom-call(bf16[64,16,128]{2,1,0:T(8,128)(2,1)} %hyena.1.in_hbm), custom_call_target="tpu_custom_call" | custom-call | tf_op jit(solution)/shard_map/scatter_rows/pallas_call | solution.py:438

commit v3 on v2

--- a/solution.py
+++ b/solution.py
@@ -114,22 +114,21 @@
 def kernel(
     q_hbm, k_hbm, v_hbm, g_hbm, filt_hbm, qt_hbm, kt_hbm, vt_hbm, gain_hbm,
     first_hbm, last_hbm, mid_hbm, back_hbm, twist_hbm,
-    out_hbm,
+    recv_y,
     q_ref, k_ref, v_ref, g_ref, filt_ref, qt_ref, kt_ref, vt_ref, gain_ref,
     first_ref, last_ref, mid_ref, back_ref, twist_ref,
-    send_x, recv_x, send_f, recv_f, send_y, recv_y,
-    input_sem, taps_sem, table_sem, out_sem, send_x_sem, recv_x_sem, send_f_sem, recv_f_sem,
-    share_send_sem, share_recv_sem, send_y_sem, recv_y_sem,
+    send_x, recv_x, send_f, recv_f, send_y, filt_spec,
+    input_sem, taps_sem, table_sem, send_x_sem, recv_x_sem, send_f_sem, recv_f_sem,
+    share_send_sem, share_recv_sem, far_sem, send_y_sem, recv_y_sem,
 ):
     me = lax.axis_index("seq")
     group = lax.axis_index("chan")
-    me_z, me_x, me_y = me // 8, (me // 2) % 4, me % 2
-
-    def partner(step):
-        dz = (step * 3) % 8
-        dx = (step // 8) % 4
-        dy = step // 32
-        return ((me_z + dz) % 8) * 8 + ((me_x + dx) % 4) * 2 + (me_y + dy) % 2
+    home, part_of = me % CHAN, me // FILTERS
+    channel = home * FILTERS + me // CHAN
+    core_peer, far_peer = group + 1 - 2 * (group % 2), (group + 2) % CHAN
+    planes = [(me // 8 + dz) % 8 * 8 for dz in (0, 4, 1, 7, 3, 5, 2, 6)]
+    highs = [(me // 4 + dx) % 2 * 4 for dx in range(2)]
+    lows = [home, home + 1 - 2 * (me % 2), (home + 2) % 4, (home + 2) % 4 + 1 - 2 * (me % 2)]
 
     def copies(pairs, sems):
         return [
@@ -159,33 +158,33 @@
 
     barrier = pltpu.get_barrier_semaphore()
 
-    def greet(step, carry):
-        pl.semaphore_signal(barrier, inc=1, device_id={"seq": partner(step)}, device_id_type=MESH)
-        return carry
-
-    lax.fori_loop(1, SEQ, greet, 0)
-    source_group = me // FILTERS
+    for low in lows:
+        for high in highs:
+            for plane in planes:
+                if low is lows[0] and high is highs[0] and plane is planes[0]:
+                    continue
+                pl.semaphore_signal(
+                    barrier, inc=1, device_id={"seq": plane + high + low}, device_id_type=MESH
+                )
+    own_filter = (home == group) & (part_of == group)
 
     def greet_source(step, carry):
         source = group * FILTERS + (me + step) % FILTERS
 
-        @pl.when(jnp.logical_not((source == me) & (source_group == group)))
+        @pl.when(jnp.logical_not((source == me) & (home == group)))
         def _():
             pl.semaphore_signal(
-                barrier, inc=1, device_id={"seq": source, "chan": source_group}, device_id_type=MESH
+                barrier, inc=1, device_id={"seq": source, "chan": home}, device_id_type=MESH
             )
 
         return carry
 
     lax.fori_loop(0, FILTERS, greet_source, 0)
-    for step in range(1, CHAN):
-        pl.semaphore_signal(
-            barrier, inc=1, device_id={"chan": (group + step) % CHAN}, device_id_type=MESH
-        )
+    for peer in (core_peer, far_peer):
+        pl.semaphore_signal(barrier, inc=1, device_id={"chan": peer}, device_id_type=MESH)
     for copy in taps_copies + table_copies:
         copy.start()
-    for copy in input_copies:
-        copy.wait()
+    input_copies[0].wait()
 
     filt_h, filt_l = split(filt_ref[...])
     pieces = [part[:, LANES * j : LANES * (j + 1)] for part in (filt_h, filt_l) for j in range(4)]
@@ -194,22 +193,25 @@
     regroup = jnp.where((row % 8 == col // 16) & (row // 8 == col % 16), 1.0, 0.0).astype(BF16)
     send_f[...] = dot(regroup, jnp.concatenate(pieces, axis=0)).astype(BF16).reshape(FILTERS, 8, LANES)
     swap = swap_matrix()
-    for m in range(4):
+    for copy in input_copies[1:]:
+        copy.wait()
+
+    def regroup_inputs(low):
         pieces = [
-            ref[16 * m : 16 * (m + 1), LANES * j : LANES * (j + 1)]
+            ref[pl.ds(pl.multiple_of(16 * low, 16), 16), LANES * j : LANES * (j + 1)]
             for ref in (q_ref, k_ref, v_ref, g_ref)
             for j in range(4)
         ]
-        mixed_rows = dot(swap, jnp.concatenate(pieces, axis=0)).astype(BF16)
-        send_x[16 * m : 16 * (m + 1)] = mixed_rows.reshape(16, 16, LANES)
-
-    own_filter = (me // FILTERS == group) & (source_group == group)
-    pl.semaphore_wait(barrier, SEQ - 1 + FILTERS + CHAN - 1 - own_filter.astype(jnp.int32))
+        rows = dot(swap, jnp.concatenate(pieces, axis=0)).astype(BF16)
+        send_x[pl.ds(16 * low, 16)] = rows.reshape(16, 16, LANES)
+
+    regroup_inputs(lows[0])
+    pl.semaphore_wait(barrier, SEQ - 1 + FILTERS + 2 - own_filter.astype(jnp.int32))
 
     def send_filter(step, carry):
         r = (me + step) % FILTERS
-        target = group * FILTERS + r
-        to_self = (target == me) & (source_group == group)
+        target = CHAN * r + group
+        to_self = (target == me) & (part_of == group)
 
         @pl.when(to_self)
         def _():
@@ -222,7 +224,7 @@
                 dst_ref=recv_f.at[me],
                 send_sem=send_f_sem,
                 recv_sem=recv_f_sem,
-                device_id={"seq": target, "chan": source_group},
+                device_id={"seq": target, "chan": part_of},
                 device_id_type=MESH,
             ).start()
 
@@ -230,35 +232,55 @@
 
     lax.fori_loop(0, FILTERS, send_filter, 0)
 
-    pltpu.make_async_copy(send_x.at[me], recv_x.at[me], recv_x_sem).start()
-
-    def send_inputs(step, carry):
-        target = partner(step)
+    pltpu.make_async_copy(send_x.at[channel], recv_x.at[me], recv_x_sem).start()
+    for low in lows:
+        if low is not lows[0]:
+            regroup_inputs(low)
+        for high in highs:
+            for plane in planes:
+                if low is lows[0] and high is highs[0] and plane is planes[0]:
+                    continue
+                pltpu.make_async_remote_copy(
+                    src_ref=send_x.at[low * FILTERS + (plane + high) // CHAN],
+                    dst_ref=recv_x.at[me],
+                    send_sem=send_x_sem,
+                    recv_sem=recv_x_sem,
+                    device_id={"seq": plane + high + low},
+                    device_id_type=MESH,
+                ).start()
+
+    def filter_part(index):
+        return recv_f.at[pl.ds(index * FILTERS, FILTERS)]
+
+    def share(index, peer, sem):
         pltpu.make_async_remote_copy(
-            src_ref=send_x.at[target],
-            dst_ref=recv_x.at[me],
-            send_sem=send_x_sem,
-            recv_sem=recv_x_sem,
-            device_id={"seq": target},
+            src_ref=filter_part(index),
+            dst_ref=filter_part(index),
+            send_sem=share_send_sem,
+            recv_sem=sem,
+            device_id={"chan": peer},
             device_id_type=MESH,
         ).start()
-        return carry
-
-    lax.fori_loop(1, SEQ, send_inputs, 0)
-
-    part = recv_f.at[pl.ds(group * FILTERS, FILTERS)]
-    pltpu.make_async_copy(part, part, recv_f_sem).wait()
-    for step in range(1, CHAN):
-        pltpu.make_async_remote_copy(
-            src_ref=part,
-            dst_ref=part,
-            send_sem=share_send_sem,
-            recv_sem=share_recv_sem,
-            device_id={"chan": (group + step) % CHAN},
-            device_id_type=MESH,
-        ).start()
+
+    pltpu.make_async_copy(filter_part(group), filter_part(group), recv_f_sem).wait()
+    share(group, far_peer, far_sem)
+    share(group, core_peer, share_recv_sem)
+    pltpu.make_async_copy(filter_part(far_peer), filter_part(far_peer), far_sem).wait()
+    share(far_peer, core_peer, share_recv_sem)
+    two = recv_f.at[pl.ds(0, 2 * FILTERS)]
+    pltpu.make_async_copy(two, two, share_recv_sem).wait()
     three = recv_f.at[pl.ds(0, (CHAN - 1) * FILTERS)]
-    pltpu.make_async_copy(three, three, share_recv_sem).wait()
+
+    for copy in taps_copies + table_copies:
+        copy.wait()
+
+    cosine, sine = twist_ref[0], twist_ref[1]
+
+    def spectrum(outer):
+        real, imag = outer[:ROWS], outer[ROWS:]
+        turned = jnp.concatenate([real * cosine + imag * sine, imag * cosine - real * sine], axis=1)
+        whole = table_right(*split(turned), mid_ref)
+        return whole[:, :LANES], whole[:, LANES:]
 
     sort_f = sort_matrix(32, 2, True)
     filt_hi, filt_lo = [], []
@@ -267,9 +289,11 @@
         rows = dot(sort_f, got).astype(BF16)
         filt_hi.append(rows[:128])
         filt_lo.append(rows[128:])
-
-    for copy in taps_copies + table_copies:
-        copy.wait()
+    filt_re, filt_im = spectrum(
+        table_left(first_ref, jnp.concatenate(filt_hi, axis=0), jnp.concatenate(filt_lo, axis=0))
+    )
+    filt_spec[0] = filt_re
+    filt_spec[1] = filt_im
 
     pltpu.make_async_copy(recv_x, recv_x, recv_x_sem).wait()
     sort_x = sort_matrix(16, 4, True)
@@ -283,12 +307,12 @@
 
     def causal_taps(signal, taps):
         return (
-            taps[0, me] * signal + taps[1, me] * delayed(signal, 1) + taps[2, me] * delayed(signal, 2)
+            taps[0, channel] * signal + taps[1, channel] * delayed(signal, 1) + taps[2, channel] * delayed(signal, 2)
         )
 
     def reverse_taps(signal, taps):
         return (
-            taps[0, me] * signal + taps[1, me] * advanced(signal, 1) + taps[2, me] * advanced(signal, 2)
+            taps[0, channel] * signal + taps[1, channel] * advanced(signal, 1) + taps[2, channel] * advanced(signal, 2)
         )
 
     short_q = causal_taps(query, qt_ref)
@@ -297,35 +321,22 @@
     product = short_k * short_v
     grad_mixed = cotangent * short_q
 
-    prod_h, prod_l = split(product)
-    grad_h, grad_l = split(grad_mixed)
-    high = jnp.concatenate([jnp.concatenate(filt_hi, axis=0), prod_h, grad_h], axis=1)
-    low = jnp.concatenate([jnp.concatenate(filt_lo, axis=0), prod_l, grad_l], axis=1)
-    outer = table_left(first_ref, high, low)
-    cosine, sine = twist_ref[0], twist_ref[1]
-
-    def spectrum(index):
-        real = outer[:ROWS, LANES * index : LANES * (index + 1)]
-        imag = outer[ROWS:, LANES * index : LANES * (index + 1)]
-        turned = jnp.concatenate([real * cosine + imag * sine, imag * cosine - real * sine], axis=1)
-        whole = table_right(*split(turned), mid_ref)
-        return whole[:, :LANES], whole[:, LANES:]
-
-    filt_re, filt_im = spectrum(0)
+    outer = table_left(first_ref, *split(jnp.concatenate([product, grad_mixed], axis=1)))
+    filt_re, filt_im = filt_spec[0], filt_spec[1]
 
     def inverse(real, imag):
         back = table_right(*split(jnp.concatenate([real, imag], axis=1)), back_ref)
         real, imag = back[:, :LANES], back[:, LANES:]
         return jnp.concatenate([real * cosine - imag * sine, imag * cosine + real * sine], axis=0)
 
-    prod_re, prod_im = spectrum(1)
+    prod_re, prod_im = spectrum(outer[:, :LANES])
     fwd = inverse(filt_re * prod_re - filt_im * prod_im, filt_re * prod_im + filt_im * prod_re)
-    grad_re, grad_im = spectrum(2)
+    grad_re, grad_im = spectrum(outer[:, LANES:])
     bwd = inverse(filt_re * grad_re + filt_im * grad_im, filt_re * grad_im - filt_im * grad_re)
     both = table_left(last_ref, *split(jnp.concatenate([fwd, bwd], axis=1)))
     causal, backward = both[:, :LANES], both[:, LANES:]
 
-    gain = gain_ref[me]
+    gain = gain_ref[channel]
     mixed = causal + gain * product
     gated = short_q * mixed
     grad_product = backward + gain * grad_mixed
@@ -340,21 +351,20 @@
         rows = jnp.concatenate([out[64 * m : 64 * (m + 1)] for out in outs], axis=0)
         send_y[16 * m : 16 * (m + 1)] = dot(sort_y, rows).astype(BF16).reshape(16, 16, LANES)
 
-    pltpu.make_async_copy(send_y.at[me], recv_y.at[me], recv_y_sem).start()
-
-    def send_outputs(step, carry):
-        target = partner(step)
-        pltpu.make_async_remote_copy(
-            src_ref=send_y.at[target],
-            dst_ref=recv_y.at[me],
-            send_sem=send_y_sem,
-            recv_sem=recv_y_sem,
-            device_id={"seq": target},
-            device_id_type=MESH,
-        ).start()
-        return carry
-
-    lax.fori_loop(1, SEQ, send_outputs, 0)
+    pltpu.make_async_copy(send_y.at[me], recv_y.at[channel], recv_y_sem).start()
+    for low in lows:
+        for high in highs:
+            for plane in planes:
+                if low is lows[0] and high is highs[0] and plane is planes[0]:
+                    continue
+                pltpu.make_async_remote_copy(
+                    src_ref=send_y.at[plane + high + low],
+                    dst_ref=recv_y.at[channel],
+                    send_sem=send_y_sem,
+                    recv_sem=recv_y_sem,
+                    device_id={"seq": plane + high + low},
+                    device_id_type=MESH,
+                ).start()
 
     sent = send_x.at[pl.ds(0, SEQ - 1)]
     pltpu.make_async_copy(sent, sent, send_x_sem).wait()
@@ -370,19 +380,13 @@
         pltpu.make_async_copy(send_f, send_f, send_f_sem).wait()
 
     pltpu.make_async_copy(recv_y, recv_y, recv_y_sem).wait()
-    result = pltpu.make_async_copy(recv_y, out_hbm, out_sem)
-    result.start()
     sent = send_y.at[pl.ds(0, SEQ - 1)]
     pltpu.make_async_copy(sent, sent, send_y_sem).wait()
-    result.wait()
-
-
-def scatter_kernel(in_hbm, *refs):
-    out_hbm, (in_ref, *out_refs), (in_sem, out_sem) = refs[:4], refs[4:9], refs[9:]
-    copy = pltpu.make_async_copy(in_hbm, in_ref, in_sem)
-    copy.start()
+
+
+def scatter_kernel(in_ref, *refs):
+    out_hbm, out_refs, out_sem = refs[:4], refs[4:8], refs[8]
     swap = swap_matrix()
-    copy.wait()
     for m in range(4):
         rows = dot(swap, in_ref[16 * m : 16 * (m + 1)].reshape(256, LANES)).astype(BF16)
         for i, ref in enumerate(out_refs):
@@ -401,6 +405,7 @@
 
 def body(q, k, v, long_filter, q_taps, k_taps, v_taps, gain, cotangent):
     constants = [jnp.asarray(table) for table in tables()]
+    vmem = pl.BlockSpec(memory_space=pltpu.VMEM)
     anywhere = pl.BlockSpec(memory_space=pl.ANY)
     block = pltpu.VMEM((SEQ, BLOCK), BF16)
     exchange = pltpu.VMEM((SEQ, 16, LANES), BF16)
@@ -408,7 +413,7 @@
         kernel,
         out_shape=jax.ShapeDtypeStruct((SEQ, 16, LANES), BF16),
         in_specs=[anywhere] * 14,
-        out_specs=anywhere,
+        out_specs=vmem,
         scratch_shapes=[block] * 4
         + [pltpu.VMEM((FILTERS, BLOCK), F32)]
         + [pltpu.SMEM((3, SEQ), F32)] * 3
@@ -424,7 +429,7 @@
             pltpu.VMEM((FILTERS, 8, LANES), BF16),
             pltpu.VMEM((SEQ, 8, LANES), BF16),
             exchange,
-            exchange,
+            pltpu.VMEM((2, ROWS, LANES), F32),
             pltpu.SemaphoreType.DMA((5,)),
             pltpu.SemaphoreType.DMA((4,)),
             pltpu.SemaphoreType.DMA((5,)),
@@ -438,9 +443,9 @@
     return pl.pallas_call(
         scatter_kernel,
         out_shape=[jax.ShapeDtypeStruct((SEQ, BLOCK), BF16)] * 4,
-        in_specs=[anywhere],
+        in_specs=[vmem],
         out_specs=[anywhere] * 4,
-        scratch_shapes=[exchange] + [block] * 4 + [pltpu.SemaphoreType.DMA, pltpu.SemaphoreType.DMA((4,))],
+        scratch_shapes=[block] * 4 + [pltpu.SemaphoreType.DMA((4,))],
         compiler_params=pltpu.CompilerParams(vmem_limit_bytes=VMEM_LIMIT),
         name="scatter_rows",
     )(arrived)

time: 41.1 us -> 40.7 us (level)
  the two profiles are of different devices: /device:TPU:16 before, /device:TPU:1 now
where the time goes in v3:
time: 40.7 us; the launch traced here: 40.1 us
  Pallas kernels  39.4 us (97%)
  between operations  0.64 us (2%)
    pallas_call x1, Pallas kernels, body(): pl.pallas_call(kernel, out_shape=jax.ShapeDtypeStruct((SEQ, 16, LANES), B...  37.5 us
    pallas_call x1, Pallas kernels, body(): pl.pallas_call(scatter_kernel, out_shape=[jax.ShapeDtypeStruct((SEQ, BLOC...  1.92 us

profile of v3, /device:TPU:1, one launch (start us, length us, event | category | flops | bytes accessed | tf_op | source)
XLA Modules:
  0.0 40.1 jit_solution(7387735455735326263)
XLA Ops:
  0.6 37.5 %hyena.1.in_ref = bf16[64,16,128]{2,1,0:T(8,128)(2,1)} custom-call(bf16[64,512]{1,0:T(8,128)(2,1)} %q_hbm.1, bf16[64,512]{1,0:T(8,128)(2,1)} %k_hbm.1, bf16[64,512]{1,0:T(8,128)(2,1)} %v_hbm.1, bf16[64,512]{1,0:T(8,128)(2,1)} %g_hbm.1, f32[16,512]{1,0:T(8,128)} %filt_hbm.1, f32[3,64]{1,0:T(4,128)} %qt_hbm.1, f32[3,64]{1,0:T(4,128)} %kt_hbm.1, ...), custom_call_target="tpu_custom_call" | custom-call | tf_op jit(solution)/shard_map/hyena/pallas_call | solution.py:412
  38.1 1.9 %scatter_rows.1 = (bf16[64,512]{1,0:T(8,128)(2,1)}, bf16[64,512]{1,0:T(8,128)(2,1)}, bf16[64,512]{1,0:T(8,128)(2,1)}, bf16[64,512]{1,0:T(8,128)(2,1)}) custom-call(bf16[64,16,128]{2,1,0:T(8,128)(2,1)} %hyena.1.in_ref), custom_call_target="tpu_custom_call" | custom-call | tf_op jit(solution)/shard_map/scatter_rows/pallas_call | solution.py:443

commit v4 on v3

--- a/solution.py
+++ b/solution.py
@@ -117,7 +117,7 @@
     recv_y,
     q_ref, k_ref, v_ref, g_ref, filt_ref, qt_ref, kt_ref, vt_ref, gain_ref,
     first_ref, last_ref, mid_ref, back_ref, twist_ref,
-    send_x, recv_x, send_f, recv_f, send_y, filt_spec,
+    send_x, recv_x, send_f, recv_f, send_y, spec,
     input_sem, taps_sem, table_sem, send_x_sem, recv_x_sem, send_f_sem, recv_f_sem,
     share_send_sem, share_recv_sem, far_sem, send_y_sem, recv_y_sem,
 ):
@@ -126,9 +126,15 @@
     home, part_of = me % CHAN, me // FILTERS
     channel = home * FILTERS + me // CHAN
     core_peer, far_peer = group + 1 - 2 * (group % 2), (group + 2) % CHAN
-    planes = [(me // 8 + dz) % 8 * 8 for dz in (0, 4, 1, 7, 3, 5, 2, 6)]
+    planes = [(me // 8 + dz) % 8 * 8 for dz in range(8)]
     highs = [(me // 4 + dx) % 2 * 4 for dx in range(2)]
     lows = [home, home + 1 - 2 * (me % 2), (home + 2) % 4, (home + 2) % 4 + 1 - 2 * (me % 2)]
+
+    def hops(dz, high, low):
+        return min(dz, 8 - dz) + (low // 2 if high == 0 else 2 - low // 2) + low % 2
+
+    steps = [(dz, high, low) for low in range(4) for high in range(2) for dz in range(8)]
+    steps = sorted(steps[1:], key=lambda step: -hops(*step))
 
     def copies(pairs, sems):
         return [
@@ -158,14 +164,9 @@
 
     barrier = pltpu.get_barrier_semaphore()
 
-    for low in lows:
-        for high in highs:
-            for plane in planes:
-                if low is lows[0] and high is highs[0] and plane is planes[0]:
-                    continue
-                pl.semaphore_signal(
-                    barrier, inc=1, device_id={"seq": plane + high + low}, device_id_type=MESH
-                )
+    for dz, high, low in steps:
+        partner = planes[dz] + highs[high] + lows[low]
+        pl.semaphore_signal(barrier, inc=1, device_id={"seq": partner}, device_id_type=MESH)
     own_filter = (home == group) & (part_of == group)
 
     def greet_source(step, carry):
@@ -196,16 +197,17 @@
     for copy in input_copies[1:]:
         copy.wait()
 
-    def regroup_inputs(low):
+    def regroup_inputs(m):
         pieces = [
-            ref[pl.ds(pl.multiple_of(16 * low, 16), 16), LANES * j : LANES * (j + 1)]
+            ref[16 * m : 16 * (m + 1), LANES * j : LANES * (j + 1)]
             for ref in (q_ref, k_ref, v_ref, g_ref)
             for j in range(4)
         ]
         rows = dot(swap, jnp.concatenate(pieces, axis=0)).astype(BF16)
-        send_x[pl.ds(16 * low, 16)] = rows.reshape(16, 16, LANES)
-
-    regroup_inputs(lows[0])
+        send_x[16 * m : 16 * (m + 1)] = rows.reshape(16, 16, LANES)
+
+    for m in range(4):
+        regroup_inputs(m)
     pl.semaphore_wait(barrier, SEQ - 1 + FILTERS + 2 - own_filter.astype(jnp.int32))
 
     def send_filter(step, carry):
@@ -233,21 +235,19 @@
     lax.fori_loop(0, FILTERS, send_filter, 0)
 
     pltpu.make_async_copy(send_x.at[channel], recv_x.at[me], recv_x_sem).start()
-    for low in lows:
-        if low is not lows[0]:
-            regroup_inputs(low)
-        for high in highs:
-            for plane in planes:
-                if low is lows[0] and high is highs[0] and plane is planes[0]:
-                    continue
-                pltpu.make_async_remote_copy(
-                    src_ref=send_x.at[low * FILTERS + (plane + high) // CHAN],
-                    dst_ref=recv_x.at[me],
-                    send_sem=send_x_sem,
-                    recv_sem=recv_x_sem,
-                    device_id={"seq": plane + high + low},
-                    device_id_type=MESH,
-                ).start()
+    def send_inputs(some):
+        for dz, high, low in some:
+            place = planes[dz] + highs[high]
+            pltpu.make_async_remote_copy(
+                src_ref=send_x.at[lows[low] * FILTERS + place // CHAN],
+                dst_ref=recv_x.at[me],
+                send_sem=send_x_sem,
+                recv_sem=recv_x_sem,
+                device_id={"seq": place + lows[low]},
+                device_id_type=MESH,
+            ).start()
+
+    send_inputs(steps)
 
     def filter_part(index):
         return recv_f.at[pl.ds(index * FILTERS, FILTERS)]
@@ -267,8 +267,6 @@
     share(group, core_peer, share_recv_sem)
     pltpu.make_async_copy(filter_part(far_peer), filter_part(far_peer), far_sem).wait()
     share(far_peer, core_peer, share_recv_sem)
-    two = recv_f.at[pl.ds(0, 2 * FILTERS)]
-    pltpu.make_async_copy(two, two, share_recv_sem).wait()
     three = recv_f.at[pl.ds(0, (CHAN - 1) * FILTERS)]
 
     for copy in taps_copies + table_copies:
@@ -282,6 +280,38 @@
         whole = table_right(*split(turned), mid_ref)
         return whole[:, :LANES], whole[:, LANES:]
 
+    pltpu.make_async_copy(recv_x, recv_x, recv_x_sem).wait()
+    sort_x = sort_matrix(16, 4, True)
+    parts = []
+    for m in range(4):
+        got = recv_x[16 * m : 16 * (m + 1)].reshape(256, LANES)
+        parts.append(dot(sort_x, got))
+    query, key, value, cotangent = (
+        jnp.concatenate([rows[64 * i : 64 * (i + 1)] for rows in parts], axis=0) for i in range(4)
+    )
+
+    def causal_taps(signal, taps):
+        return (
+            taps[0, channel] * signal + taps[1, channel] * delayed(signal, 1) + taps[2, channel] * delayed(signal, 2)
+        )
+
+    def reverse_taps(signal, taps):
+        return (
+            taps[0, channel] * signal + taps[1, channel] * advanced(signal, 1) + taps[2, channel] * advanced(signal, 2)
+        )
+
+    short_q = causal_taps(query, qt_ref)
+    short_k = causal_taps(key, kt_ref)
+    short_v = causal_taps(value, vt_ref)
+    product = short_k * short_v
+    grad_mixed = cotangent * short_q
+
+    outer = table_left(first_ref, *split(jnp.concatenate([product, grad_mixed], axis=1)))
+    spec[0], spec[1] = spectrum(outer[:, :LANES])
+    spec[2], spec[3] = spectrum(outer[:, LANES:])
+
+    two = recv_f.at[pl.ds(0, 2 * FILTERS)]
+    pltpu.make_async_copy(two, two, share_recv_sem).wait()
     sort_f = sort_matrix(32, 2, True)
     filt_hi, filt_lo = [], []
     for m in range(2):
@@ -292,46 +322,15 @@
     filt_re, filt_im = spectrum(
         table_left(first_ref, jnp.concatenate(filt_hi, axis=0), jnp.concatenate(filt_lo, axis=0))
     )
-    filt_spec[0] = filt_re
-    filt_spec[1] = filt_im
-
-    pltpu.make_async_copy(recv_x, recv_x, recv_x_sem).wait()
-    sort_x = sort_matrix(16, 4, True)
-    parts = []
-    for m in range(4):
-        got = recv_x[16 * m : 16 * (m + 1)].reshape(256, LANES)
-        parts.append(dot(sort_x, got))
-    query, key, value, cotangent = (
-        jnp.concatenate([rows[64 * i : 64 * (i + 1)] for rows in parts], axis=0) for i in range(4)
-    )
-
-    def causal_taps(signal, taps):
-        return (
-            taps[0, channel] * signal + taps[1, channel] * delayed(signal, 1) + taps[2, channel] * delayed(signal, 2)
-        )
-
-    def reverse_taps(signal, taps):
-        return (
-            taps[0, channel] * signal + taps[1, channel] * advanced(signal, 1) + taps[2, channel] * advanced(signal, 2)
-        )
-
-    short_q = causal_taps(query, qt_ref)
-    short_k = causal_taps(key, kt_ref)
-    short_v = causal_taps(value, vt_ref)
-    product = short_k * short_v
-    grad_mixed = cotangent * short_q
-
-    outer = table_left(first_ref, *split(jnp.concatenate([product, grad_mixed], axis=1)))
-    filt_re, filt_im = filt_spec[0], filt_spec[1]
 
     def inverse(real, imag):
         back = table_right(*split(jnp.concatenate([real, imag], axis=1)), back_ref)
         real, imag = back[:, :LANES], back[:, LANES:]
         return jnp.concatenate([real * cosine - imag * sine, imag * cosine + real * sine], axis=0)
 
-    prod_re, prod_im = spectrum(outer[:, :LANES])
+    prod_re, prod_im = spec[0], spec[1]
     fwd = inverse(filt_re * prod_re - filt_im * prod_im, filt_re * prod_im + filt_im * prod_re)
-    grad_re, grad_im = spectrum(outer[:, LANES:])
+    grad_re, grad_im = spec[2], spec[3]
     bwd = inverse(filt_re * grad_re + filt_im * grad_im, filt_re * grad_im - filt_im * grad_re)
     both = table_left(last_ref, *split(jnp.concatenate([fwd, bwd], axis=1)))
     causal, backward = both[:, :LANES], both[:, LANES:]
@@ -352,19 +351,16 @@
         send_y[16 * m : 16 * (m + 1)] = dot(sort_y, rows).astype(BF16).reshape(16, 16, LANES)
 
     pltpu.make_async_copy(send_y.at[me], recv_y.at[channel], recv_y_sem).start()
-    for low in lows:
-        for high in highs:
-            for plane in planes:
-                if low is lows[0] and high is highs[0] and plane is planes[0]:
-                    continue
-                pltpu.make_async_remote_copy(
-                    src_ref=send_y.at[plane + high + low],
-                    dst_ref=recv_y.at[channel],
-                    send_sem=send_y_sem,
-                    recv_sem=recv_y_sem,
-                    device_id={"seq": plane + high + low},
-                    device_id_type=MESH,
-                ).start()
+    for dz, high, low in steps:
+        target = planes[dz] + highs[high] + lows[low]
+        pltpu.make_async_remote_copy(
+            src_ref=send_y.at[target],
+            dst_ref=recv_y.at[channel],
+            send_sem=send_y_sem,
+            recv_sem=recv_y_sem,
+            device_id={"seq": target},
+            device_id_type=MESH,
+        ).start()
 
     sent = send_x.at[pl.ds(0, SEQ - 1)]
     pltpu.make_async_copy(sent, sent, send_x_sem).wait()
@@ -429,7 +425,7 @@
             pltpu.VMEM((FILTERS, 8, LANES), BF16),
             pltpu.VMEM((SEQ, 8, LANES), BF16),
             exchange,
-            pltpu.VMEM((2, ROWS, LANES), F32),
+            pltpu.VMEM((4, ROWS, LANES), F32),
             pltpu.SemaphoreType.DMA((5,)),
             pltpu.SemaphoreType.DMA((4,)),
             pltpu.SemaphoreType.DMA((5,)),

time: 40.7 us -> 38.6 us (0.948); the launches traced: 40.1 us -> 38.5 us
  Pallas kernels: 39.4 us -> 37.8 us
    pallas_call x1, Pallas kernels: 37.5 us -> 35.9 us  [body(): pl.pallas_call(kernel, out_shape=jax.ShapeDtypeStruct((SEQ, 16, LANES), B...]
where the time goes in v4:
time: 38.6 us; the launch traced here: 38.5 us
  Pallas kernels  37.8 us (98%)
  between operations  0.64 us (2%)
    pallas_call x1, Pallas kernels, body(): pl.pallas_call(kernel, out_shape=jax.ShapeDtypeStruct((SEQ, 16, LANES), B...  35.9 us
    pallas_call x1, Pallas kernels, body(): pl.pallas_call(scatter_kernel, out_shape=[jax.ShapeDtypeStruct((SEQ, BLOC...  1.92 us

profile of v4, /device:TPU:1, one launch (start us, length us, event | category | flops | bytes accessed | tf_op | source)
XLA Modules:
  0.0 38.5 jit_solution(6267732184128125084)
XLA Ops:
  0.6 35.9 %hyena.1.in_ref = bf16[64,16,128]{2,1,0:T(8,128)(2,1)} custom-call(bf16[64,512]{1,0:T(8,128)(2,1)} %q_hbm.1, bf16[64,512]{1,0:T(8,128)(2,1)} %k_hbm.1, bf16[64,512]{1,0:T(8,128)(2,1)} %v_hbm.1, bf16[64,512]{1,0:T(8,128)(2,1)} %g_hbm.1, f32[16,512]{1,0:T(8,128)} %filt_hbm.1, f32[3,64]{1,0:T(4,128)} %qt_hbm.1, f32[3,64]{1,0:T(4,128)} %kt_hbm.1, ...), custom_call_target="tpu_custom_call" | custom-call | tf_op jit(solution)/shard_map/hyena/pallas_call | solution.py:408
  36.6 1.9 %scatter_rows.1 = (bf16[64,512]{1,0:T(8,128)(2,1)}, bf16[64,512]{1,0:T(8,128)(2,1)}, bf16[64,512]{1,0:T(8,128)(2,1)}, bf16[64,512]{1,0:T(8,128)(2,1)}) custom-call(bf16[64,16,128]{2,1,0:T(8,128)(2,1)} %hyena.1.in_ref), custom_call_target="tpu_custom_call" | custom-call | tf_op jit(solution)/shard_map/scatter_rows/pallas_call | solution.py:439

commit v5 on v4

--- a/solution.py
+++ b/solution.py
@@ -95,20 +95,24 @@
     return jnp.where(hit, 1.0, 0.0).astype(BF16)
 
 
-def delayed(value, steps):
+def delayed(value):
     lane = lax.broadcasted_iota(jnp.int32, (ROWS, LANES), 1)
     row = lax.broadcasted_iota(jnp.int32, (ROWS, LANES), 0)
-    turned = pltpu.roll(value, steps, 1)
-    above = jnp.where(row == 0, 0.0, pltpu.roll(turned, 1, 0))
-    return jnp.where(lane < steps, above, turned)
-
-
-def advanced(value, steps):
+    above = jnp.where(row == 0, 0.0, pltpu.roll(value, 1, 0))
+    return [
+        pltpu.roll(jnp.where(lane >= LANES - steps, above, value), steps, 1) for steps in (1, 2)
+    ]
+
+
+def advanced(value):
     lane = lax.broadcasted_iota(jnp.int32, (ROWS, LANES), 1)
     row = lax.broadcasted_iota(jnp.int32, (ROWS, LANES), 0)
-    turned = pltpu.roll(value, LANES - steps, 1)
-    below = jnp.where(row == ROWS - 1, 0.0, pltpu.roll(turned, ROWS - 1, 0))
-    return jnp.where(lane >= LANES - steps, below, turned)
+    below = jnp.where(row == ROWS - 1, 0.0, pltpu.roll(value, ROWS - 1, 0))
+    return [pltpu.roll(jnp.where(lane < steps, below, value), LANES - steps, 1) for steps in (1, 2)]
+
+
+def side_by_side(left, right):
+    return jnp.concatenate([left, right], axis=1)
 
 
 def kernel(
@@ -164,23 +168,26 @@
 
     barrier = pltpu.get_barrier_semaphore()
 
+    own_filter = (home == group) & (part_of == group)
+
+    for step in range(1, FILTERS):
+        source = group * FILTERS + (me + step) % FILTERS
+        pl.semaphore_signal(
+            barrier, inc=1, device_id={"seq": source, "chan": home}, device_id_type=MESH
+        )
+
+    @pl.when(jnp.logical_not(own_filter))
+    def _():
+        pl.semaphore_signal(
+            barrier,
+            inc=1,
+            device_id={"seq": group * FILTERS + me % FILTERS, "chan": home},
+            device_id_type=MESH,
+        )
+
     for dz, high, low in steps:
         partner = planes[dz] + highs[high] + lows[low]
         pl.semaphore_signal(barrier, inc=1, device_id={"seq": partner}, device_id_type=MESH)
-    own_filter = (home == group) & (part_of == group)
-
-    def greet_source(step, carry):
-        source = group * FILTERS + (me + step) % FILTERS
-
-        @pl.when(jnp.logical_not((source == me) & (home == group)))
-        def _():
-            pl.semaphore_signal(
-                barrier, inc=1, device_id={"seq": source, "chan": home}, device_id_type=MESH
-            )
-
-        return carry
-
-    lax.fori_loop(0, FILTERS, greet_source, 0)
     for peer in (core_peer, far_peer):
         pl.semaphore_signal(barrier, inc=1, device_id={"chan": peer}, device_id_type=MESH)
     for copy in taps_copies + table_copies:
@@ -197,42 +204,43 @@
     for copy in input_copies[1:]:
         copy.wait()
 
-    def regroup_inputs(m):
-        pieces = [
-            ref[16 * m : 16 * (m + 1), LANES * j : LANES * (j + 1)]
-            for ref in (q_ref, k_ref, v_ref, g_ref)
-            for j in range(4)
-        ]
-        rows = dot(swap, jnp.concatenate(pieces, axis=0)).astype(BF16)
-        send_x[16 * m : 16 * (m + 1)] = rows.reshape(16, 16, LANES)
-
-    for m in range(4):
-        regroup_inputs(m)
+    def gather(m):
+        return jnp.concatenate(
+            [
+                ref[16 * m : 16 * (m + 1), LANES * j : LANES * (j + 1)]
+                for ref in (q_ref, k_ref, v_ref, g_ref)
+                for j in range(4)
+            ],
+            axis=0,
+        )
+
+    for m in (0, 2):
+        rows = dot(swap, side_by_side(gather(m), gather(m + 1))).astype(BF16)
+        send_x[16 * m : 16 * (m + 1)] = rows[:, :LANES].reshape(16, 16, LANES)
+        send_x[16 * (m + 1) : 16 * (m + 2)] = rows[:, LANES:].reshape(16, 16, LANES)
+
     pl.semaphore_wait(barrier, SEQ - 1 + FILTERS + 2 - own_filter.astype(jnp.int32))
 
-    def send_filter(step, carry):
-        r = (me + step) % FILTERS
-        target = CHAN * r + group
-        to_self = (target == me) & (part_of == group)
-
-        @pl.when(to_self)
-        def _():
-            pltpu.make_async_copy(send_f.at[r], recv_f.at[me], recv_f_sem).start()
-
-        @pl.when(jnp.logical_not(to_self))
-        def _():
-            pltpu.make_async_remote_copy(
-                src_ref=send_f.at[r],
-                dst_ref=recv_f.at[me],
-                send_sem=send_f_sem,
-                recv_sem=recv_f_sem,
-                device_id={"seq": target, "chan": part_of},
-                device_id_type=MESH,
-            ).start()
-
-        return carry
-
-    lax.fori_loop(0, FILTERS, send_filter, 0)
+    def send_filter(r):
+        pltpu.make_async_remote_copy(
+            src_ref=send_f.at[r],
+            dst_ref=recv_f.at[me],
+            send_sem=send_f_sem,
+            recv_sem=recv_f_sem,
+            device_id={"seq": CHAN * r + group, "chan": part_of},
+            device_id_type=MESH,
+        ).start()
+
+    for step in sorted(range(1, FILTERS), key=lambda step: -min(step, FILTERS - step)):
+        send_filter((me // CHAN + step) % FILTERS)
+
+    @pl.when(own_filter)
+    def _():
+        pltpu.make_async_copy(send_f.at[me // CHAN], recv_f.at[me], recv_f_sem).start()
+
+    @pl.when(jnp.logical_not(own_filter))
+    def _():
+        send_filter(me // CHAN)
 
     pltpu.make_async_copy(send_x.at[channel], recv_x.at[me], recv_x_sem).start()
     def send_inputs(some):
@@ -274,31 +282,32 @@
 
     cosine, sine = twist_ref[0], twist_ref[1]
 
-    def spectrum(outer):
-        real, imag = outer[:ROWS], outer[ROWS:]
-        turned = jnp.concatenate([real * cosine + imag * sine, imag * cosine - real * sine], axis=1)
-        whole = table_right(*split(turned), mid_ref)
-        return whole[:, :LANES], whole[:, LANES:]
+    def twist(real, imag):
+        return side_by_side(real * cosine + imag * sine, imag * cosine - real * sine)
+
+    def untwist(back):
+        real, imag = back[:, :LANES], back[:, LANES:]
+        return jnp.concatenate([real * cosine - imag * sine, imag * cosine + real * sine], axis=0)
 
     pltpu.make_async_copy(recv_x, recv_x, recv_x_sem).wait()
     sort_x = sort_matrix(16, 4, True)
     parts = []
-    for m in range(4):
-        got = recv_x[16 * m : 16 * (m + 1)].reshape(256, LANES)
-        parts.append(dot(sort_x, got))
+    for m in (0, 2):
+        pair = [recv_x[16 * n : 16 * (n + 1)].reshape(256, LANES) for n in (m, m + 1)]
+        rows = dot(sort_x, side_by_side(*pair))
+        parts += [rows[:, :LANES], rows[:, LANES:]]
     query, key, value, cotangent = (
         jnp.concatenate([rows[64 * i : 64 * (i + 1)] for rows in parts], axis=0) for i in range(4)
     )
 
+    def short_filter(signal, taps, near, far):
+        return taps[0, channel] * signal + taps[1, channel] * near + taps[2, channel] * far
+
     def causal_taps(signal, taps):
-        return (
-            taps[0, channel] * signal + taps[1, channel] * delayed(signal, 1) + taps[2, channel] * delayed(signal, 2)
-        )
+        return short_filter(signal, taps, *delayed(signal))
 
     def reverse_taps(signal, taps):
-        return (
-            taps[0, channel] * signal + taps[1, channel] * advanced(signal, 1) + taps[2, channel] * advanced(signal, 2)
-        )
+        return short_filter(signal, taps, *advanced(signal))
 
     short_q = causal_taps(query, qt_ref)
     short_k = causal_taps(key, kt_ref)
@@ -307,32 +316,43 @@
     grad_mixed = cotangent * short_q
 
     outer = table_left(first_ref, *split(jnp.concatenate([product, grad_mixed], axis=1)))
-    spec[0], spec[1] = spectrum(outer[:, :LANES])
-    spec[2], spec[3] = spectrum(outer[:, LANES:])
+    turned = jnp.concatenate(
+        [
+            twist(outer[:ROWS, :LANES], outer[ROWS:, :LANES]),
+            twist(outer[:ROWS, LANES:], outer[ROWS:, LANES:]),
+        ],
+        axis=0,
+    )
+    spec[...] = table_right(*split(turned), mid_ref)
 
     two = recv_f.at[pl.ds(0, 2 * FILTERS)]
     pltpu.make_async_copy(two, two, share_recv_sem).wait()
     sort_f = sort_matrix(32, 2, True)
-    filt_hi, filt_lo = [], []
-    for m in range(2):
-        got = recv_f[32 * m : 32 * (m + 1)].reshape(256, LANES)
-        rows = dot(sort_f, got).astype(BF16)
-        filt_hi.append(rows[:128])
-        filt_lo.append(rows[128:])
-    filt_re, filt_im = spectrum(
-        table_left(first_ref, jnp.concatenate(filt_hi, axis=0), jnp.concatenate(filt_lo, axis=0))
-    )
-
-    def inverse(real, imag):
-        back = table_right(*split(jnp.concatenate([real, imag], axis=1)), back_ref)
-        real, imag = back[:, :LANES], back[:, LANES:]
-        return jnp.concatenate([real * cosine - imag * sine, imag * cosine + real * sine], axis=0)
-
-    prod_re, prod_im = spec[0], spec[1]
-    fwd = inverse(filt_re * prod_re - filt_im * prod_im, filt_re * prod_im + filt_im * prod_re)
-    grad_re, grad_im = spec[2], spec[3]
-    bwd = inverse(filt_re * grad_re + filt_im * grad_im, filt_re * grad_im - filt_im * grad_re)
-    both = table_left(last_ref, *split(jnp.concatenate([fwd, bwd], axis=1)))
+    pair = [recv_f[32 * m : 32 * (m + 1)].reshape(256, LANES) for m in range(2)]
+    rows = dot(sort_f, side_by_side(*pair)).astype(BF16)
+    outer = table_left(
+        first_ref,
+        jnp.concatenate([rows[:128, :LANES], rows[:128, LANES:]], axis=0),
+        jnp.concatenate([rows[128:, :LANES], rows[128:, LANES:]], axis=0),
+    )
+    filt = table_right(*split(twist(outer[:ROWS], outer[ROWS:])), mid_ref)
+    filt_re, filt_im = filt[:, :LANES], filt[:, LANES:]
+    prod_re, prod_im = spec[:ROWS, :LANES], spec[:ROWS, LANES:]
+    grad_re, grad_im = spec[ROWS:, :LANES], spec[ROWS:, LANES:]
+    both = jnp.concatenate(
+        [
+            side_by_side(
+                filt_re * prod_re - filt_im * prod_im, filt_re * prod_im + filt_im * prod_re
+            ),
+            side_by_side(
+                filt_re * grad_re + filt_im * grad_im, filt_re * grad_im - filt_im * grad_re
+            ),
+        ],
+        axis=0,
+    )
+    back = table_right(*split(both), back_ref)
+    both = side_by_side(untwist(back[:ROWS]), untwist(back[ROWS:]))
+    both = table_left(last_ref, *split(both))
     causal, backward = both[:, :LANES], both[:, LANES:]
 
     gain = gain_ref[channel]
@@ -346,9 +366,14 @@
         reverse_taps(grad_product * short_k, vt_ref).astype(BF16),
     ]
     sort_y = sort_matrix(16, 4, False)
-    for m in range(4):
-        rows = jnp.concatenate([out[64 * m : 64 * (m + 1)] for out in outs], axis=0)
-        send_y[16 * m : 16 * (m + 1)] = dot(sort_y, rows).astype(BF16).reshape(16, 16, LANES)
+
+    def chunk(m):
+        return jnp.concatenate([out[64 * m : 64 * (m + 1)] for out in outs], axis=0)
+
+    for m in (0, 2):
+        rows = dot(sort_y, side_by_side(chunk(m), chunk(m + 1))).astype(BF16)
+        send_y[16 * m : 16 * (m + 1)] = rows[:, :LANES].reshape(16, 16, LANES)
+        send_y[16 * (m + 1) : 16 * (m + 2)] = rows[:, LANES:].reshape(16, 16, LANES)
 
     pltpu.make_async_copy(send_y.at[me], recv_y.at[channel], recv_y_sem).start()
     for dz, high, low in steps:
@@ -380,9 +405,12 @@
     pltpu.make_async_copy(sent, sent, send_y_sem).wait()
 
 
-def scatter_kernel(in_ref, *refs):
-    out_hbm, out_refs, out_sem = refs[:4], refs[4:8], refs[8]
+def scatter_kernel(in_hbm, *refs):
+    out_hbm, in_ref, out_refs, in_sem, out_sem = refs[:4], refs[4], refs[5:9], refs[9], refs[10]
+    load = pltpu.make_async_copy(in_hbm, in_ref, in_sem)
+    load.start()
     swap = swap_matrix()
+    load.wait()
     for m in range(4):
         rows = dot(swap, in_ref[16 * m : 16 * (m + 1)].reshape(256, LANES)).astype(BF16)
         for i, ref in enumerate(out_refs):
@@ -401,15 +429,14 @@
 
 def body(q, k, v, long_filter, q_taps, k_taps, v_taps, gain, cotangent):
     constants = [jnp.asarray(table) for table in tables()]
-    vmem = pl.BlockSpec(memory_space=pltpu.VMEM)
-    anywhere = pl.BlockSpec(memory_space=pl.ANY)
+    hbm = pl.BlockSpec(memory_space=pltpu.HBM)
     block = pltpu.VMEM((SEQ, BLOCK), BF16)
     exchange = pltpu.VMEM((SEQ, 16, LANES), BF16)
     arrived = pl.pallas_call(
         kernel,
         out_shape=jax.ShapeDtypeStruct((SEQ, 16, LANES), BF16),
-        in_specs=[anywhere] * 14,
-        out_specs=vmem,
+        in_specs=[hbm] * 14,
+        out_specs=hbm,
         scratch_shapes=[block] * 4
         + [pltpu.VMEM((FILTERS, BLOCK), F32)]
         + [pltpu.SMEM((3, SEQ), F32)] * 3
@@ -425,7 +452,7 @@
             pltpu.VMEM((FILTERS, 8, LANES), BF16),
             pltpu.VMEM((SEQ, 8, LANES), BF16),
             exchange,
-            pltpu.VMEM((4, ROWS, LANES), F32),
+            pltpu.VMEM((2 * ROWS, 2 * LANES), F32),
             pltpu.SemaphoreType.DMA((5,)),
             pltpu.SemaphoreType.DMA((4,)),
             pltpu.SemaphoreType.DMA((5,)),
@@ -439,9 +466,11 @@
     return pl.pallas_call(
         scatter_kernel,
         out_shape=[jax.ShapeDtypeStruct((SEQ, BLOCK), BF16)] * 4,
-        in_specs=[vmem],
-        out_specs=[anywhere] * 4,
-        scratch_shapes=[block] * 4 + [pltpu.SemaphoreType.DMA((4,))],
+        in_specs=[hbm],
+        out_specs=[hbm] * 4,
+        scratch_shapes=[exchange]
+        + [block] * 4
+        + [pltpu.SemaphoreType.DMA, pltpu.SemaphoreType.DMA((4,))],
         compiler_params=pltpu.CompilerParams(vmem_limit_bytes=VMEM_LIMIT),
         name="scatter_rows",
     )(arrived)

time: 38.6 us -> 37.3 us (0.966)
  Pallas kernels: 37.8 us -> 36.5 us
    pallas_call x1, Pallas kernels: 35.9 us -> 34.6 us  [body(): pl.pallas_call(kernel, out_shape=jax.ShapeDtypeStruct((SEQ, 16, LANES), B...]
where the time goes in v5:
time: 37.3 us; the launch traced here: 37.1 us
  Pallas kernels  36.5 us (98%)
  between operations  0.64 us (2%)
    pallas_call x1, Pallas kernels, body(): pl.pallas_call(kernel, out_shape=jax.ShapeDtypeStruct((SEQ, 16, LANES), B...  34.6 us
    pallas_call x1, Pallas kernels, body(): pl.pallas_call(scatter_kernel, out_shape=[jax.ShapeDtypeStruct((SEQ, BLOC...  1.92 us

profile of v5, /device:TPU:1, one launch (start us, length us, event | category | flops | bytes accessed | tf_op | source)
XLA Modules:
  0.0 37.1 jit_solution(7335237807769909252)
XLA Ops:
  0.6 34.6 %hyena.1.in_hbm = bf16[64,16,128]{2,1,0:T(8,128)(2,1)} custom-call(bf16[64,512]{1,0:T(8,128)(2,1)} %q_hbm.1, bf16[64,512]{1,0:T(8,128)(2,1)} %k_hbm.1, bf16[64,512]{1,0:T(8,128)(2,1)} %v_hbm.1, bf16[64,512]{1,0:T(8,128)(2,1)} %g_hbm.1, f32[16,512]{1,0:T(8,128)} %filt_hbm.1, f32[3,64]{1,0:T(4,128)} %qt_hbm.1, f32[3,64]{1,0:T(4,128)} %kt_hbm.1, ...), custom_call_target="tpu_custom_call" | custom-call | tf_op jit(solution)/shard_map/hyena/pallas_call | solution.py:435
  35.2 1.9 %scatter_rows.1 = (bf16[64,512]{1,0:T(8,128)(2,1)}, bf16[64,512]{1,0:T(8,128)(2,1)}, bf16[64,512]{1,0:T(8,128)(2,1)}, bf16[64,512]{1,0:T(8,128)(2,1)}) custom-call(bf16[64,16,128]{2,1,0:T(8,128)(2,1)} %hyena.1.in_hbm), custom_call_target="tpu_custom_call" | custom-call | tf_op jit(solution)/shard_map/scatter_rows/pallas_call | solution.py:466

commit v6 on v5

v6 whole, which is shorter than its diff:
```python
import functools

import jax
import jax.numpy as jnp
import ml_dtypes
import numpy as np
from jax import lax
from jax.experimental import pallas as pl
from jax.experimental.pallas import tpu as pltpu
from jax.sharding import PartitionSpec as P

SEQ = 64
CHAN = 4
BLOCK = 512
LANES = 128
ROWS = 256
FILTERS = SEQ // CHAN
FULL = 2 * ROWS * LANES
VMEM_LIMIT = 60 * 1024 * 1024

BF16 = jnp.bfloat16
F32 = jnp.float32
MESH = pl.DeviceIdType.MESH


def split_table(table):
    high = table.astype(ml_dtypes.bfloat16)
    low = (table - high.astype(np.float64)).astype(ml_dtypes.bfloat16)
    return high, low


@functools.lru_cache(maxsize=None)
def tables():
    k1 = np.arange(ROWS)
    a = np.arange(ROWS)
    b = np.arange(LANES)
    outer = 2 * np.pi * ((a[None, :] * (2 * k1[:, None] + 1)) % 1024) / 1024.0
    first = np.concatenate([np.cos(outer), -np.sin(outer)], axis=0)
    last = first.T * (2.0 / FULL)
    twist = 2 * np.pi * (b[None, :] * (2 * k1[:, None] + 1)) / (2.0 * FULL)
    inner = 2 * np.pi * ((b[None, :] * b[:, None]) % LANES) / LANES
    cosine, sine = np.cos(inner), np.sin(inner)
    mid = np.block([[cosine, -sine], [sine, cosine]])
    back = np.block([[cosine, sine], [-sine, cosine]])
    first_h, first_l = split_table(first)
    last_h, last_l = split_table(last)
    mid_h, mid_l = split_table(mid)
    back_h, back_l = split_table(back)
    return (
        np.stack([first_h, first_l]),
        np.stack([last_h, last_l]),
        np.stack([mid_h, mid_l]),
        np.stack([back_h, back_l]),
        np.stack([np.cos(twist), np.sin(twist)]).astype(np.float32),
    )


def split(value):
    high = value.astype(BF16)
    low = (value - high.astype(F32)).astype(BF16)
    return high, low


def dot(left, right):
    return jnp.dot(left, right, preferred_element_type=F32)


def table_left(table, high, low):
    table_h, table_l = table[0], table[1]
    left = jnp.concatenate([table_h, table_h, table_l], axis=1)
    return dot(left, jnp.concatenate([high, low, high], axis=0))


def table_right(high, low, table):
    table_h, table_l = table[0], table[1]
    right = jnp.concatenate([table_h, table_h, table_l], axis=0)
    return dot(jnp.concatenate([high, low, high], axis=1), right)


def swap_matrix(outer):
    row = lax.broadcasted_iota(jnp.int32, (256, 256), 0)
    col = lax.broadcasted_iota(jnp.int32, (256, 256), 1)
    inner = 256 // outer
    return jnp.where(col == row % inner * outer + row // inner, 1.0, 0.0).astype(BF16)


def sort_matrix(outer, kinds, to_kinds):
    size = outer * kinds * 4
    row = lax.broadcasted_iota(jnp.int32, (size, size), 0)
    col = lax.broadcasted_iota(jnp.int32, (size, size), 1)
    by_kind, by_shard = (row, col) if to_kinds else (col, row)
    kind = by_kind // (outer * 4)
    shard = (by_kind // 4) % outer
    hit = by_shard == shard * (kinds * 4) + kind * 4 + by_kind % 4
    return jnp.where(hit, 1.0, 0.0).astype(BF16)


def delayed(value):
    lane = lax.broadcasted_iota(jnp.int32, (ROWS, LANES), 1)
    row = lax.broadcasted_iota(jnp.int32, (ROWS, LANES), 0)
    above = jnp.where(row == 0, 0.0, pltpu.roll(value, 1, 0))
    return [
        pltpu.roll(jnp.where(lane >= LANES - steps, above, value), steps, 1) for steps in (1, 2)
    ]


def advanced(value):
    lane = lax.broadcasted_iota(jnp.int32, (ROWS, LANES), 1)
    row = lax.broadcasted_iota(jnp.int32, (ROWS, LANES), 0)
    below = jnp.where(row == ROWS - 1, 0.0, pltpu.roll(value, ROWS - 1, 0))
    return [pltpu.roll(jnp.where(lane < steps, below, value), LANES - steps, 1) for steps in (1, 2)]


def put_groups(target, rows):
    target[0:32] = rows[:, :LANES].astype(BF16).reshape(32, 8, LANES)
    target[32:64] = rows[:, LANES:].astype(BF16).reshape(32, 8, LANES)


def get_groups(source):
    return side_by_side(*[source[32 * m : 32 * (m + 1)].reshape(256, LANES) for m in range(2)])


def stack_groups(rows):
    return [
        jnp.concatenate([rows[at : at + 128, :LANES], rows[at : at + 128, LANES:]], axis=0)
        for at in (0, 128)
    ]


def side_by_side(left, right):
    return jnp.concatenate([left, right], axis=1)


def kernel(
    q_hbm, k_hbm, v_hbm, g_hbm, filt_hbm, qt_hbm, kt_hbm, vt_hbm, gain_hbm,
    first_hbm, last_hbm, mid_hbm, back_hbm, twist_hbm,
    recv_c, recv_d,
    q_ref, k_ref, v_ref, g_ref, filt_ref, qt_ref, kt_ref, vt_ref, gain_ref,
    first_ref, last_ref, mid_ref, back_ref, twist_ref,
    send_a, recv_a, send_b, recv_b, send_f, recv_f, send_c, send_d,
    filt_spec, short_k, short_v, mixed_ref, grad_ref,
    input_sem, taps_sem, table_sem,
    in_a_sem, in_b_sem, out_c_sem, out_d_sem,
    send_f_sem, recv_f_sem, share_send_sem, share_recv_sem,
):
    me = lax.axis_index("seq")
    group = lax.axis_index("chan")
    home, core = me % CHAN, group % 2
    own_filter = (home == group) & (me // (2 * FILTERS) == core)
    half = me // (2 * FILTERS)
    channel = home * FILTERS + me // CHAN
    core_peer = group + 1 - 2 * core
    planes = [(me // 8 + dz) % 8 * 8 for dz in range(8)]
    highs = [(me // 4 + dx) % 2 * 4 for dx in range(2)]
    lows = [home, home + 1 - 2 * (me % 2), (home + 2) % 4, (home + 2) % 4 + 1 - 2 * (me % 2)]

    def hops(dz, high, low):
        return min(dz, 8 - dz) + (low // 2 if high == 0 else 2 - low // 2) + low % 2

    steps = [(dz, high, low) for low in range(4) for high in range(2) for dz in range(8)]
    steps = sorted(steps[1:], key=lambda step: -hops(*step))

    def copies(pairs, sems):
        return [
            pltpu.make_async_copy(source, target, sems.at[index])
            for index, (source, target) in enumerate(pairs)
        ]

    input_copies = copies(
        [(filt_hbm, filt_ref), (q_hbm, q_ref), (k_hbm, k_ref), (v_hbm, v_ref), (g_hbm, g_ref)],
        input_sem,
    )
    taps_copies = copies(
        [(qt_hbm, qt_ref), (kt_hbm, kt_ref), (vt_hbm, vt_ref), (gain_hbm, gain_ref)], taps_sem
    )
    table_copies = copies(
        [
            (first_hbm, first_ref),
            (mid_hbm, mid_ref),
            (twist_hbm, twist_ref),
            (back_hbm, back_ref),
            (last_hbm, last_ref),
        ],
        table_sem,
    )
    for copy in input_copies:
        copy.start()

    barrier = pltpu.get_barrier_semaphore()


    for step in range(1, 2 * FILTERS):
        source = core * 2 * FILTERS + (me + step) % (2 * FILTERS)
        pl.semaphore_signal(
            barrier, inc=1, device_id={"seq": source, "chan": home}, device_id_type=MESH
        )

    @pl.when(jnp.logical_not(own_filter))
    def _():
        source = core * 2 * FILTERS + me % (2 * FILTERS)
        pl.semaphore_signal(
            barrier, inc=1, device_id={"seq": source, "chan": home}, device_id_type=MESH
        )

    for dz, high, low in steps:
        partner = planes[dz] + highs[high] + lows[low]
        pl.semaphore_signal(barrier, inc=1, device_id={"seq": partner}, device_id_type=MESH)
    pl.semaphore_signal(barrier, inc=1, device_id={"chan": core_peer}, device_id_type=MESH)
    for copy in taps_copies + table_copies:
        copy.start()
    input_copies[0].wait()

    filt_h, filt_l = split(filt_ref[...])
    pieces = [part[:, LANES * j : LANES * (j + 1)] for part in (filt_h, filt_l) for j in range(4)]
    row = lax.broadcasted_iota(jnp.int32, (128, 128), 0)
    col = lax.broadcasted_iota(jnp.int32, (128, 128), 1)
    regroup = jnp.where((row % 8 == col // 16) & (row // 8 == col % 16), 1.0, 0.0).astype(BF16)
    send_f[...] = dot(regroup, jnp.concatenate(pieces, axis=0)).astype(BF16).reshape(FILTERS, 8, LANES)
    swap = swap_matrix(32)
    for copy in input_copies[1:]:
        copy.wait()
    for target, refs in ((send_a, (k_ref, v_ref)), (send_b, (q_ref, g_ref))):
        groups = [
            jnp.concatenate(
                [
                    ref[32 * m : 32 * (m + 1), LANES * j : LANES * (j + 1)]
                    for ref in refs
                    for j in range(4)
                ],
                axis=0,
            )
            for m in range(2)
        ]
        put_groups(target, dot(swap, side_by_side(*groups)))

    pl.semaphore_wait(barrier, SEQ - 1 + 2 * FILTERS + 1 - own_filter.astype(jnp.int32))

    def send_filter(r, far):
        pltpu.make_async_remote_copy(
            src_ref=send_f.at[r],
            dst_ref=recv_f.at[me],
            send_sem=send_f_sem,
            recv_sem=recv_f_sem,
            device_id={"seq": CHAN * r + group, "chan": (group // 2 + far) % 2 * 2 + half},
            device_id_type=MESH,
        ).start()

    for step in sorted(range(FILTERS), key=lambda step: -min(step, FILTERS - step)):
        send_filter((me // CHAN + step) % FILTERS, 1)
        if step > 0:
            send_filter((me // CHAN + step) % FILTERS, 0)

    @pl.when(own_filter)
    def _():
        pltpu.make_async_copy(send_f.at[me // CHAN], recv_f.at[me], recv_f_sem).start()

    @pl.when(jnp.logical_not(own_filter))
    def _():
        send_filter(me // CHAN, 0)

    def send_inputs(source, target, sems):
        pltpu.make_async_copy(source.at[channel], target.at[me], sems.at[1]).start()
        for dz, high, low in steps:
            place = planes[dz] + highs[high]
            pltpu.make_async_remote_copy(
                src_ref=source.at[lows[low] * FILTERS + place // CHAN],
                dst_ref=target.at[me],
                send_sem=sems.at[0],
                recv_sem=sems.at[1],
                device_id={"seq": place + lows[low]},
                device_id_type=MESH,
            ).start()

    def send_outputs(source, target, sems):
        pltpu.make_async_copy(source.at[me], target.at[channel], sems.at[1]).start()
        for dz, high, low in steps:
            place = planes[dz] + highs[high] + lows[low]
            pltpu.make_async_remote_copy(
                src_ref=source.at[place],
                dst_ref=target.at[channel],
                send_sem=sems.at[0],
                recv_sem=sems.at[1],
                device_id={"seq": place},
                device_id_type=MESH,
            ).start()

    send_inputs(send_a, recv_a, in_a_sem)
    send_inputs(send_b, recv_b, in_b_sem)

    own_half = recv_f.at[pl.ds(core * 2 * FILTERS, 2 * FILTERS)]
    pltpu.make_async_copy(own_half, own_half, recv_f_sem).wait()
    pltpu.make_async_remote_copy(
        src_ref=own_half,
        dst_ref=own_half,
        send_sem=share_send_sem,
        recv_sem=share_recv_sem,
        device_id={"chan": core_peer},
        device_id_type=MESH,
    ).start()

    for copy in taps_copies + table_copies:
        copy.wait()

    cosine, sine = twist_ref[0], twist_ref[1]

    def twist(real, imag):
        return side_by_side(real * cosine + imag * sine, imag * cosine - real * sine)

    def untwist(back):
        real, imag = back[:, :LANES], back[:, LANES:]
        return jnp.concatenate([real * cosine - imag * sine, imag * cosine + real * sine], axis=0)

    def short_filter(signal, taps, near, far):
        return taps[0, channel] * signal + taps[1, channel] * near + taps[2, channel] * far

    def causal_taps(signal, taps):
        return short_filter(signal, taps, *delayed(signal))

    def reverse_taps(signal, taps):
        return short_filter(signal, taps, *advanced(signal))

    sort_in = sort_matrix(32, 2, True)
    sort_out = sort_matrix(32, 2, False)
    gain = gain_ref[channel]

    pltpu.make_async_copy(recv_a, recv_a, in_a_sem.at[1]).wait()
    key, value = stack_groups(dot(sort_in, get_groups(recv_a)))
    short_k[...] = causal_taps(key, kt_ref)
    short_v[...] = causal_taps(value, vt_ref)
    product = short_k[...] * short_v[...]
    prod_h, prod_l = split(product)
    pltpu.make_async_copy(own_half, own_half, share_recv_sem).wait()
    filt_h, filt_l = stack_groups(dot(sort_in, get_groups(recv_f)).astype(BF16))
    outer = table_left(first_ref, side_by_side(filt_h, prod_h), side_by_side(filt_l, prod_l))
    turned = jnp.concatenate(
        [
            twist(outer[:ROWS, :LANES], outer[ROWS:, :LANES]),
            twist(outer[:ROWS, LANES:], outer[ROWS:, LANES:]),
        ],
        axis=0,
    )
    spec = table_right(*split(turned), mid_ref)
    filt_re, filt_im = spec[:ROWS, :LANES], spec[:ROWS, LANES:]
    prod_re, prod_im = spec[ROWS:, :LANES], spec[ROWS:, LANES:]
    filt_spec[...] = spec[:ROWS]

    def inverse(real, imag):
        back = table_right(*split(side_by_side(real, imag)), back_ref)
        return table_left(last_ref, *split(untwist(back)))

    causal = inverse(filt_re * prod_re - filt_im * prod_im, filt_re * prod_im + filt_im * prod_re)
    mixed_ref[...] = causal + gain * product

    pltpu.make_async_copy(recv_b, recv_b, in_b_sem.at[1]).wait()
    query, cotangent = stack_groups(dot(sort_in, get_groups(recv_b)))
    short_q = causal_taps(query, qt_ref)
    mixed = mixed_ref[...]
    grad_ref[...] = cotangent * short_q

    def leave(target, first, second):
        first, second = first.astype(BF16), second.astype(BF16)
        groups = [
            jnp.concatenate([first[at : at + 128], second[at : at + 128]], axis=0)
            for at in (0, 128)
        ]
        put_groups(target, dot(sort_out, side_by_side(*groups)))

    leave(send_c, short_q * mixed, reverse_taps(cotangent * mixed, qt_ref))
    send_outputs(send_c, recv_c, out_c_sem)

    grad_mixed = grad_ref[...]
    outer = table_left(first_ref, *split(grad_mixed))
    spec = table_right(*split(twist(outer[:ROWS], outer[ROWS:])), mid_ref)
    grad_re, grad_im = spec[:, :LANES], spec[:, LANES:]
    filt_re, filt_im = filt_spec[:, :LANES], filt_spec[:, LANES:]
    backward = inverse(
        filt_re * grad_re + filt_im * grad_im, filt_re * grad_im - filt_im * grad_re
    )
    grad_product = backward + gain * grad_mixed
    leave(
        send_d,
        reverse_taps(grad_product * short_v[...], kt_ref),
        reverse_taps(grad_product * short_k[...], vt_ref),
    )
    send_outputs(send_d, recv_d, out_d_sem)

    for source, sems in (
        (send_a, in_a_sem), (send_b, in_b_sem), (send_c, out_c_sem), (send_d, out_d_sem)
    ):
        sent = source.at[pl.ds(0, SEQ - 1)]
        pltpu.make_async_copy(sent, sent, sems.at[0]).wait()
    pltpu.make_async_copy(own_half, own_half, share_send_sem).wait()
    pltpu.make_async_copy(send_f, send_f, send_f_sem).wait()

    @pl.when(own_filter)
    def _():
        some = send_f.at[pl.ds(0, FILTERS - 1)]
        pltpu.make_async_copy(some, some, send_f_sem).wait()

    @pl.when(jnp.logical_not(own_filter))
    def _():
        pltpu.make_async_copy(send_f, send_f, send_f_sem).wait()

    pltpu.make_async_copy(recv_c, recv_c, out_c_sem.at[1]).wait()
    pltpu.make_async_copy(recv_d, recv_d, out_d_sem.at[1]).wait()


def scatter_kernel(c_hbm, d_hbm, *refs):
    out_hbm, in_refs, out_refs, in_sem, out_sem = refs[:4], refs[4:6], refs[6:10], refs[10], refs[11]
    loads = [
        pltpu.make_async_copy(hbm, ref, in_sem.at[i])
        for i, (hbm, ref) in enumerate(zip((c_hbm, d_hbm), in_refs))
    ]
    for load in loads:
        load.start()
    swap = swap_matrix(8)
    stores = []
    for n in range(2):
        loads[n].wait()
        rows = dot(swap, get_groups(in_refs[n])).astype(BF16)
        for i in range(2):
            ref = out_refs[2 * n + i]
            for j in range(4):
                at = (4 * i + j) * 32
                for m in range(2):
                    ref[32 * m : 32 * (m + 1), LANES * j : LANES * (j + 1)] = rows[
                        at : at + 32, LANES * m : LANES * (m + 1)
                    ]
            stores.append(pltpu.make_async_copy(ref, out_hbm[2 * n + i], out_sem.at[2 * n + i]))
            stores[-1].start()
    for store in stores:
        store.wait()


def body(q, k, v, long_filter, q_taps, k_taps, v_taps, gain, cotangent):
    constants = [jnp.asarray(table) for table in tables()]
    hbm = pl.BlockSpec(memory_space=pltpu.HBM)
    block = pltpu.VMEM((SEQ, BLOCK), BF16)
    wave = pltpu.VMEM((SEQ, 8, LANES), BF16)
    signal = pltpu.VMEM((ROWS, LANES), F32)
    arrived = pl.pallas_call(
        kernel,
        out_shape=[jax.ShapeDtypeStruct((SEQ, 8, LANES), BF16)] * 2,
        in_specs=[hbm] * 14,
        out_specs=[hbm] * 2,
        scratch_shapes=[block] * 4
        + [pltpu.VMEM((FILTERS, BLOCK), F32)]
        + [pltpu.SMEM((3, SEQ), F32)] * 3
        + [pltpu.SMEM((SEQ,), F32)]
        + [
            pltpu.VMEM((2, 512, 256), BF16),
            pltpu.VMEM((2, 256, 512), BF16),
            pltpu.VMEM((2, 256, 256), BF16),
            pltpu.VMEM((2, 256, 256), BF16),
            pltpu.VMEM((2, ROWS, LANES), F32),
            wave,
            wave,
            wave,
            wave,
            pltpu.VMEM((FILTERS, 8, LANES), BF16),
            wave,
            wave,
            wave,
            pltpu.VMEM((ROWS, 2 * LANES), F32),
        ]
        + [signal] * 4
        + [
            pltpu.SemaphoreType.DMA((5,)),
            pltpu.SemaphoreType.DMA((4,)),
            pltpu.SemaphoreType.DMA((5,)),
        ]
        + [pltpu.SemaphoreType.DMA((2,))] * 4
        + [pltpu.SemaphoreType.DMA] * 4,
        compiler_params=pltpu.CompilerParams(
            collective_id=0, has_side_effects=True, vmem_limit_bytes=VMEM_LIMIT
        ),
        name="hyena",
    )(q, k, v, cotangent, long_filter, q_taps, k_taps, v_taps, gain, *constants)
    return pl.pallas_call(
        scatter_kernel,
        out_shape=[jax.ShapeDtypeStruct((SEQ, BLOCK), BF16)] * 4,
        in_specs=[hbm] * 2,
        out_specs=[hbm] * 4,
        scratch_shapes=[wave] * 2
        + [block] * 4
        + [pltpu.SemaphoreType.DMA((2,)), pltpu.SemaphoreType.DMA((4,))],
        compiler_params=pltpu.CompilerParams(vmem_limit_bytes=VMEM_LIMIT),
        name="scatter_rows",
    )(*arrived)


def solution(mesh):
    in_specs = (
        P("chan", "seq"),
        P("chan", "seq"),
        P("chan", "seq"),
        P("chan", "seq"),
        P(None, "chan"),
        P(None, "chan"),
        P(None, "chan"),
        P("chan"),
        P("chan", "seq"),
    )
    out_specs = (P("chan", "seq"),) * 4
    return jax.shard_map(body, mesh=mesh, in_specs=in_specs, out_specs=out_specs, check_vma=False)
```

time: 37.3 us -> 36.5 us (0.979)
  Pallas kernels: 36.5 us -> 35.8 us
    pallas_call x1, Pallas kernels: 34.6 us -> 33.8 us  [body(): pl.pallas_call(kernel, out_shape=[jax.ShapeDtypeStruct((SEQ, 8, LANES), B...]
where the time goes in v6:
time: 36.5 us; the launch traced here: 36.4 us
  Pallas kernels  35.8 us (98%)
  between operations  0.64 us (2%)
    pallas_call x1, Pallas kernels, body(): pl.pallas_call(kernel, out_shape=[jax.ShapeDtypeStruct((SEQ, 8, LANES), B...  33.8 us
    pallas_call x1, Pallas kernels, body(): pl.pallas_call(scatter_kernel, out_shape=[jax.ShapeDtypeStruct((SEQ, BLOC...  2.02 us

profile of v6, /device:TPU:1, one launch (start us, length us, event | category | flops | bytes accessed | tf_op | source)
XLA Modules:
  0.0 36.4 jit_solution(8860674565923911004)
XLA Ops:
  0.6 33.8 %hyena.1 = (bf16[64,8,128]{2,1,0:T(8,128)(2,1)}, bf16[64,8,128]{2,1,0:T(8,128)(2,1)}) custom-call(bf16[64,512]{1,0:T(8,128)(2,1)} %q_hbm.1, bf16[64,512]{1,0:T(8,128)(2,1)} %k_hbm.1, bf16[64,512]{1,0:T(8,128)(2,1)} %v_hbm.1, bf16[64,512]{1,0:T(8,128)(2,1)} %g_hbm.1, f32[16,512]{1,0:T(8,128)} %filt_hbm.1, f32[3,64]{1,0:T(4,128)} %qt_hbm.1, f32[3,64]{1,0:T(4,128)} %kt_hbm.1, ...), custom_call_target="tpu_custom_call" | custom-call | tf_op jit(solution)/shard_map/hyena/pallas_call | solution.py:441
  34.4 2.0 %scatter_rows.1 = (bf16[64,512]{1,0:T(8,128)(2,1)}, bf16[64,512]{1,0:T(8,128)(2,1)}, bf16[64,512]{1,0:T(8,128)(2,1)}, bf16[64,512]{1,0:T(8,128)(2,1)}) custom-call(bf16[64,8,128]{2,1,0:T(8,128)(2,1)} %get-tuple-element.6.c_hbm, bf16[64,8,128]{2,1,0:T(8,128)(2,1)} %get-tuple-element.7.d_hbm), custom_call_target="tpu_custom_call" | custom-call | tf_op jit(solution)/shard_map/scatter_rows/pallas_call | solution.py:479

commit v7 on v6

--- a/solution.py
+++ b/solution.py
@@ -146,8 +146,9 @@
     me = lax.axis_index("seq")
     group = lax.axis_index("chan")
     home, core = me % CHAN, group % 2
-    own_filter = (home == group) & (me // (2 * FILTERS) == core)
-    half = me // (2 * FILTERS)
+    at_home = home == group
+    across = home == (group + 2) % CHAN
+    direct = home % 2 == core
     channel = home * FILTERS + me // CHAN
     core_peer = group + 1 - 2 * core
     planes = [(me // 8 + dz) % 8 * 8 for dz in range(8)]
@@ -189,18 +190,13 @@
     barrier = pltpu.get_barrier_semaphore()
 
 
-    for step in range(1, 2 * FILTERS):
-        source = core * 2 * FILTERS + (me + step) % (2 * FILTERS)
-        pl.semaphore_signal(
-            barrier, inc=1, device_id={"seq": source, "chan": home}, device_id_type=MESH
-        )
-
-    @pl.when(jnp.logical_not(own_filter))
-    def _():
-        source = core * 2 * FILTERS + me % (2 * FILTERS)
-        pl.semaphore_signal(
-            barrier, inc=1, device_id={"seq": source, "chan": home}, device_id_type=MESH
-        )
+    @pl.when(across)
+    def _():
+        for dz, high, low in steps + [(0, 0, 0)]:
+            source = planes[dz] + highs[high] + lows[low]
+            pl.semaphore_signal(
+                barrier, inc=1, device_id={"seq": source, "chan": home}, device_id_type=MESH
+            )
 
     for dz, high, low in steps:
         partner = planes[dz] + highs[high] + lows[low]
@@ -233,30 +229,31 @@
         ]
         put_groups(target, dot(swap, side_by_side(*groups)))
 
-    pl.semaphore_wait(barrier, SEQ - 1 + 2 * FILTERS + 1 - own_filter.astype(jnp.int32))
-
-    def send_filter(r, far):
+    pl.semaphore_wait(barrier, SEQ - 1 + FILTERS + 1)
+
+    def send_filter(r, target_group):
         pltpu.make_async_remote_copy(
             src_ref=send_f.at[r],
             dst_ref=recv_f.at[me],
             send_sem=send_f_sem,
             recv_sem=recv_f_sem,
-            device_id={"seq": CHAN * r + group, "chan": (group // 2 + far) % 2 * 2 + half},
+            device_id={"seq": CHAN * r + group, "chan": target_group},
             device_id_type=MESH,
         ).start()
 
     for step in sorted(range(FILTERS), key=lambda step: -min(step, FILTERS - step)):
-        send_filter((me // CHAN + step) % FILTERS, 1)
+        row = (me // CHAN + step) % FILTERS
+        send_filter(row, (group + 2) % CHAN)
         if step > 0:
-            send_filter((me // CHAN + step) % FILTERS, 0)
-
-    @pl.when(own_filter)
+            send_filter(row, group)
+
+    @pl.when(at_home)
     def _():
         pltpu.make_async_copy(send_f.at[me // CHAN], recv_f.at[me], recv_f_sem).start()
 
-    @pl.when(jnp.logical_not(own_filter))
-    def _():
-        send_filter(me // CHAN, 0)
+    @pl.when(jnp.logical_not(at_home))
+    def _():
+        send_filter(me // CHAN, group)
 
     def send_inputs(source, target, sems):
         pltpu.make_async_copy(source.at[channel], target.at[me], sems.at[1]).start()
@@ -287,16 +284,17 @@
     send_inputs(send_a, recv_a, in_a_sem)
     send_inputs(send_b, recv_b, in_b_sem)
 
-    own_half = recv_f.at[pl.ds(core * 2 * FILTERS, 2 * FILTERS)]
-    pltpu.make_async_copy(own_half, own_half, recv_f_sem).wait()
-    pltpu.make_async_remote_copy(
-        src_ref=own_half,
-        dst_ref=own_half,
-        send_sem=share_send_sem,
-        recv_sem=share_recv_sem,
-        device_id={"chan": core_peer},
-        device_id_type=MESH,
-    ).start()
+    @pl.when(direct)
+    def _():
+        pltpu.make_async_copy(recv_f, recv_f, recv_f_sem).wait()
+        pltpu.make_async_remote_copy(
+            src_ref=recv_f,
+            dst_ref=recv_f,
+            send_sem=share_send_sem,
+            recv_sem=share_recv_sem,
+            device_id={"chan": core_peer},
+            device_id_type=MESH,
+        ).start()
 
     for copy in taps_copies + table_copies:
         copy.wait()
@@ -329,7 +327,11 @@
     short_v[...] = causal_taps(value, vt_ref)
     product = short_k[...] * short_v[...]
     prod_h, prod_l = split(product)
-    pltpu.make_async_copy(own_half, own_half, share_recv_sem).wait()
+
+    @pl.when(jnp.logical_not(direct))
+    def _():
+        pltpu.make_async_copy(recv_f, recv_f, share_recv_sem).wait()
+
     filt_h, filt_l = stack_groups(dot(sort_in, get_groups(recv_f)).astype(BF16))
     outer = table_left(first_ref, side_by_side(filt_h, prod_h), side_by_side(filt_l, prod_l))
     turned = jnp.concatenate(
@@ -366,13 +368,13 @@
         put_groups(target, dot(sort_out, side_by_side(*groups)))
 
     leave(send_c, short_q * mixed, reverse_taps(cotangent * mixed, qt_ref))
-    send_outputs(send_c, recv_c, out_c_sem)
 
     grad_mixed = grad_ref[...]
     outer = table_left(first_ref, *split(grad_mixed))
     spec = table_right(*split(twist(outer[:ROWS], outer[ROWS:])), mid_ref)
     grad_re, grad_im = spec[:, :LANES], spec[:, LANES:]
     filt_re, filt_im = filt_spec[:, :LANES], filt_spec[:, LANES:]
+    send_outputs(send_c, recv_c, out_c_sem)
     backward = inverse(
         filt_re * grad_re + filt_im * grad_im, filt_re * grad_im - filt_im * grad_re
     )
@@ -389,17 +391,20 @@
     ):
         sent = source.at[pl.ds(0, SEQ - 1)]
         pltpu.make_async_copy(sent, sent, sems.at[0]).wait()
-    pltpu.make_async_copy(own_half, own_half, share_send_sem).wait()
     pltpu.make_async_copy(send_f, send_f, send_f_sem).wait()
 
-    @pl.when(own_filter)
+    @pl.when(at_home)
     def _():
         some = send_f.at[pl.ds(0, FILTERS - 1)]
         pltpu.make_async_copy(some, some, send_f_sem).wait()
 
-    @pl.when(jnp.logical_not(own_filter))
+    @pl.when(jnp.logical_not(at_home))
     def _():
         pltpu.make_async_copy(send_f, send_f, send_f_sem).wait()
+
+    @pl.when(direct)
+    def _():
+        pltpu.make_async_copy(recv_f, recv_f, share_send_sem).wait()
 
     pltpu.make_async_copy(recv_c, recv_c, out_c_sem.at[1]).wait()
     pltpu.make_async_copy(recv_d, recv_d, out_d_sem.at[1]).wait()

time: 36.5 us -> 35.5 us (0.973)
  Pallas kernels: 35.8 us -> 34.7 us
    pallas_call x1, Pallas kernels: 33.8 us -> 32.7 us  [body(): pl.pallas_call(kernel, out_shape=[jax.ShapeDtypeStruct((SEQ, 8, LANES), B...]
where the time goes in v7:
time: 35.5 us; the launch traced here: 35.4 us
  Pallas kernels  34.7 us (98%)
  between operations  0.64 us (2%)
    pallas_call x1, Pallas kernels, body(): pl.pallas_call(kernel, out_shape=[jax.ShapeDtypeStruct((SEQ, 8, LANES), B...  32.7 us
    pallas_call x1, Pallas kernels, body(): pl.pallas_call(scatter_kernel, out_shape=[jax.ShapeDtypeStruct((SEQ, BLOC...  2.02 us

profile of v7, /device:TPU:1, one launch (start us, length us, event | category | flops | bytes accessed | tf_op | source)
XLA Modules:
  0.0 35.4 jit_solution(36420715752648184)
XLA Ops:
  0.6 32.7 %hyena.1 = (bf16[64,8,128]{2,1,0:T(8,128)(2,1)}, bf16[64,8,128]{2,1,0:T(8,128)(2,1)}) custom-call(bf16[64,512]{1,0:T(8,128)(2,1)} %q_hbm.1, bf16[64,512]{1,0:T(8,128)(2,1)} %k_hbm.1, bf16[64,512]{1,0:T(8,128)(2,1)} %v_hbm.1, bf16[64,512]{1,0:T(8,128)(2,1)} %g_hbm.1, f32[16,512]{1,0:T(8,128)} %filt_hbm.1, f32[3,64]{1,0:T(4,128)} %qt_hbm.1, f32[3,64]{1,0:T(4,128)} %kt_hbm.1, ...), custom_call_target="tpu_custom_call" | custom-call | tf_op jit(solution)/shard_map/hyena/pallas_call | solution.py:446
  33.3 2.0 %scatter_rows.1 = (bf16[64,512]{1,0:T(8,128)(2,1)}, bf16[64,512]{1,0:T(8,128)(2,1)}, bf16[64,512]{1,0:T(8,128)(2,1)}, bf16[64,512]{1,0:T(8,128)(2,1)}) custom-call(bf16[64,8,128]{2,1,0:T(8,128)(2,1)} %get-tuple-element.6.c_hbm, bf16[64,8,128]{2,1,0:T(8,128)(2,1)} %get-tuple-element.7.d_hbm), custom_call_target="tpu_custom_call" | custom-call | tf_op jit(solution)/shard_map/scatter_rows/pallas_call | solution.py:484

commit v8 on v7

--- a/solution.py
+++ b/solution.py
@@ -197,10 +197,17 @@
             pl.semaphore_signal(
                 barrier, inc=1, device_id={"seq": source, "chan": home}, device_id_type=MESH
             )
-
-    for dz, high, low in steps:
-        partner = planes[dz] + highs[high] + lows[low]
-        pl.semaphore_signal(barrier, inc=1, device_id={"seq": partner}, device_id_type=MESH)
+            if (dz, high, low) != (0, 0, 0):
+                pl.semaphore_signal(
+                    barrier, inc=1, device_id={"seq": source}, device_id_type=MESH
+                )
+
+    @pl.when(jnp.logical_not(across))
+    def _():
+        for dz, high, low in steps:
+            partner = planes[dz] + highs[high] + lows[low]
+            pl.semaphore_signal(barrier, inc=1, device_id={"seq": partner}, device_id_type=MESH)
+
     pl.semaphore_signal(barrier, inc=1, device_id={"chan": core_peer}, device_id_type=MESH)
     for copy in taps_copies + table_copies:
         copy.start()

time: 35.5 us -> 35.3 us (level)
  no operation moved by 1% of the time
where the time goes in v8:
time: 35.3 us; the launch traced here: 35.1 us
  Pallas kernels  34.4 us (97%)
  between operations  0.64 us (2%)
    pallas_call x1, Pallas kernels, body(): pl.pallas_call(kernel, out_shape=[jax.ShapeDtypeStruct((SEQ, 8, LANES), B...  32.4 us
    pallas_call x1, Pallas kernels, body(): pl.pallas_call(scatter_kernel, out_shape=[jax.ShapeDtypeStruct((SEQ, BLOC...  2.02 us

profile of v8, /device:TPU:1, one launch (start us, length us, event | category | flops | bytes accessed | tf_op | source)
XLA Modules:
  0.0 35.1 jit_solution(16574741498444010253)
XLA Ops:
  0.6 32.4 %hyena.1 = (bf16[64,8,128]{2,1,0:T(8,128)(2,1)}, bf16[64,8,128]{2,1,0:T(8,128)(2,1)}) custom-call(bf16[64,512]{1,0:T(8,128)(2,1)} %q_hbm.1, bf16[64,512]{1,0:T(8,128)(2,1)} %k_hbm.1, bf16[64,512]{1,0:T(8,128)(2,1)} %v_hbm.1, bf16[64,512]{1,0:T(8,128)(2,1)} %g_hbm.1, f32[16,512]{1,0:T(8,128)} %filt_hbm.1, f32[3,64]{1,0:T(4,128)} %qt_hbm.1, f32[3,64]{1,0:T(4,128)} %kt_hbm.1, ...), custom_call_target="tpu_custom_call" | custom-call | tf_op jit(solution)/shard_map/hyena/pallas_call | solution.py:453
  33.1 2.0 %scatter_rows.1 = (bf16[64,512]{1,0:T(8,128)(2,1)}, bf16[64,512]{1,0:T(8,128)(2,1)}, bf16[64,512]{1,0:T(8,128)(2,1)}, bf16[64,512]{1,0:T(8,128)(2,1)}) custom-call(bf16[64,8,128]{2,1,0:T(8,128)(2,1)} %get-tuple-element.6.c_hbm, bf16[64,8,128]{2,1,0:T(8,128)(2,1)} %get-tuple-element.7.d_hbm), custom_call_target="tpu_custom_call" | custom-call | tf_op jit(solution)/shard_map/scatter_rows/pallas_call | solution.py:491

commit v9 on v8

--- a/solution.py
+++ b/solution.py
@@ -151,7 +151,8 @@
     direct = home % 2 == core
     channel = home * FILTERS + me // CHAN
     core_peer = group + 1 - 2 * core
-    planes = [(me // 8 + dz) % 8 * 8 for dz in range(8)]
+    turn = group % 2 * 6 + 1
+    planes = [(me // 8 + dz * turn) % 8 * 8 for dz in range(8)]
     highs = [(me // 4 + dx) % 2 * 4 for dx in range(2)]
     lows = [home, home + 1 - 2 * (me % 2), (home + 2) % 4, (home + 2) % 4 + 1 - 2 * (me % 2)]
 

time: 35.3 us -> 35.2 us (level)
  no operation moved by 1% of the time
where the time goes in v9:
time: 35.2 us; the launch traced here: 35 us
  Pallas kernels  34.3 us (97%)
  between operations  0.64 us (2%)
    pallas_call x1, Pallas kernels, body(): pl.pallas_call(kernel, out_shape=[jax.ShapeDtypeStruct((SEQ, 8, LANES), B...  32.3 us
    pallas_call x1, Pallas kernels, body(): pl.pallas_call(scatter_kernel, out_shape=[jax.ShapeDtypeStruct((SEQ, BLOC...  2.02 us

profile of v9, /device:TPU:1, one launch (start us, length us, event | category | flops | bytes accessed | tf_op | source)
XLA Modules:
  0.0 35.0 jit_solution(12107281763381740379)
XLA Ops:
  0.6 32.3 %hyena.1 = (bf16[64,8,128]{2,1,0:T(8,128)(2,1)}, bf16[64,8,128]{2,1,0:T(8,128)(2,1)}) custom-call(bf16[64,512]{1,0:T(8,128)(2,1)} %q_hbm.1, bf16[64,512]{1,0:T(8,128)(2,1)} %k_hbm.1, bf16[64,512]{1,0:T(8,128)(2,1)} %v_hbm.1, bf16[64,512]{1,0:T(8,128)(2,1)} %g_hbm.1, f32[16,512]{1,0:T(8,128)} %filt_hbm.1, f32[3,64]{1,0:T(4,128)} %qt_hbm.1, f32[3,64]{1,0:T(4,128)} %kt_hbm.1, ...), custom_call_target="tpu_custom_call" | custom-call | tf_op jit(solution)/shard_map/hyena/pallas_call | solution.py:454
  33.0 2.0 %scatter_rows.1 = (bf16[64,512]{1,0:T(8,128)(2,1)}, bf16[64,512]{1,0:T(8,128)(2,1)}, bf16[64,512]{1,0:T(8,128)(2,1)}, bf16[64,512]{1,0:T(8,128)(2,1)}) custom-call(bf16[64,8,128]{2,1,0:T(8,128)(2,1)} %get-tuple-element.6.c_hbm, bf16[64,8,128]{2,1,0:T(8,128)(2,1)} %get-tuple-element.7.d_hbm), custom_call_target="tpu_custom_call" | custom-call | tf_op jit(solution)/shard_map/scatter_rows/pallas_call | solution.py:492
